TPU v7x, 32 devices: a whole 2x2x4 slice. The times are simulated.
32 devices in a mesh: slab: 8 (over z, y), px: 2 (over x), py: 2 (over core).
Axes of the slice: x: 2, y: 2, z: 4, core: 2. Of those that a mesh axis runs over, the one named last changes fastest.
Arguments:
- source: float32 [32, 4, 256, 256], P('slab', None, 'px', 'py'), may hold values from -6 to 6
- phase: float32 [32, 256, 256], P('slab', 'px', 'py'), may hold values from 0.3 to 2.8
- attenuation: float32 [32, 256, 256], P('slab', 'px', 'py'), may hold values from 0.003125 to 0.08
- pml_level: int32 [256, 256], P('px', 'py'), may hold values from 0 to 3
- recv_values: float32 [2, 2, 4, 4096], P('px', 'py', None, 'slab'), may hold values from -8 to 8
- recv_slab: int32 [2, 2, 4096, 1], P('px', 'py', 'slab'), may hold values from 0 to 7; in each aligned block of 512 rows (0 to 511, 512 to 1023, ..., all dimensions but the last counted through in order) at most 64 rows name the same one
- recv_lateral: int32 [2, 2, 4096], P('px', 'py', 'slab'), may hold values from 0 to 16383
- recv_layer: int32 [2, 2, 4096], P('px', 'py', 'slab'), may hold values from 0 to 3
Outputs:
- correction: float32 [32, 4, 256, 256], P('slab', None, 'px', 'py')
Inputs may be any that keep to these rules, and one draw needn't show every extreme that they name: `recv_slab`: among the rows of one device, at most 64 receivers name the same slab, a bound that some block reaches of them.
All inputs are finite; a program needn't handle non-finite values.
Results may differ from a plain program's by a relative error of at most 0.000034.
Values sent between devices are 32-bit elements; how exact they have to be, the bound alone decides.
A program may use at most 128 MiB of HBM per device.

v0:
```python
import jax
import jax.numpy as jnp
from jax import lax
from jax.sharding import PartitionSpec as P


def from_behind(array, axis, by):
    count = lax.axis_size(axis)
    pairs = [(i, i + by) for i in range(count) if 0 <= i + by < count]
    return lax.ppermute(array, axis, pairs)


def padded_2(block, sides, width):
    for axis, dim in sides:
        count = lax.axis_size(axis)
        forward = [(i, i + 1) for i in range(count - 1)]
        backward = [(target, source) for source, target in forward]
        low = lax.ppermute(
            lax.slice_in_dim(block, block.shape[dim] - width, None, axis=dim), axis, forward
        )
        high = lax.ppermute(lax.slice_in_dim(block, 0, width, axis=dim), axis, backward)
        block = jnp.concatenate([low, block, high], axis=dim)
    return block


def advance(state, layer):
    real_part, imag_part, prod_real, prod_imag = state
    rate_real, rate_imag, force_layer = layer
    new_real = rate_real * real_part - rate_imag * imag_part + force_layer[:, 0]
    new_imag = rate_real * imag_part + rate_imag * real_part + force_layer[:, 1]
    next_real = rate_real * prod_real - rate_imag * prod_imag
    next_imag = rate_real * prod_imag + rate_imag * prod_real
    return (
        (new_real, new_imag, next_real, next_imag),
        (jnp.stack([new_real, new_imag], axis=1), next_real, next_imag),
    )


def shards(source, phase, attenuation, pml_level, recv_values, recv_slab, recv_lateral, recv_layer):
    layers, components, width_x, width_y = source.shape
    shot_count = components // 2
    slab_count = lax.axis_size("slab")
    depth_total = layers * slab_count
    plane_size = width_x * width_y
    rows_here = recv_values.shape[3]
    capacity = rows_here // min(8, slab_count)
    values = recv_values[0, 0]
    target_slab = recv_slab[0, 0, :, 0]
    position = recv_layer[0, 0] * (components * plane_size) + recv_lateral[0, 0]
    one_hot = (target_slab[:, None] == jnp.arange(slab_count, dtype=jnp.int32)[None, :]).astype(
        jnp.int32
    )
    ranking = jnp.sum((jnp.cumsum(one_hot, axis=0) - one_hot) * one_hot, axis=1)
    target_slot = target_slab * capacity + ranking
    send_values = (
        jnp.zeros((components, slab_count * capacity), jnp.float32).at[:, target_slot].set(values)
    )
    send_places = jnp.zeros((slab_count * capacity,), jnp.int32).at[target_slot].set(position)
    got_values, got_places = (
        lax.all_to_all(
            send_values.reshape(components, slab_count, capacity),
            "slab",
            split_axis=1,
            concat_axis=1,
            tiled=True,
        ),
        lax.all_to_all(
            send_places.reshape(1, slab_count, capacity),
            "slab",
            split_axis=1,
            concat_axis=1,
            tiled=True,
        ),
    )
    inject_values = got_values.reshape(components, slab_count * capacity)
    inject_places = got_places.reshape(slab_count * capacity)
    offsets = (jnp.arange(components, dtype=jnp.int32) * plane_size)[:, None]
    flat_index = (inject_places[None, :] + offsets).reshape(-1)
    forcing = source.reshape(-1).at[flat_index].add(inject_values.reshape(-1))
    fields = forcing.reshape(layers, shot_count, 2, width_x, width_y)
    damping = attenuation + 0.5 / depth_total * pml_level.astype(jnp.float32)[None, :, :]
    amplitude = jnp.exp(-damping)
    real_mult = amplitude * jnp.cos(phase)
    imag_mult = amplitude * jnp.sin(phase)
    zeros = jnp.zeros((shot_count, width_x, width_y), jnp.float32)
    ones_plane = jnp.ones((width_x, width_y), jnp.float32)
    zero_plane = jnp.zeros((width_x, width_y), jnp.float32)
    start_state = (zeros, zeros, ones_plane, zero_plane)
    final_down, down_parts = lax.scan(advance, start_state, (real_mult, imag_mult, fields))
    final_up, up_parts = lax.scan(
        advance, start_state, (real_mult, imag_mult, fields), reverse=True
    )
    local_down, down_real, down_imag = down_parts
    local_up, up_real, up_imag = up_parts
    total_down = (down_real[-1], down_imag[-1], local_down[-1][:, 0], local_down[-1][:, 1])
    total_up = (up_real[0], up_imag[0], local_up[0][:, 0], local_up[0][:, 1])

    def relay_turn(turn_index, carry):
        enter_real, enter_imag, below_real, below_imag = carry
        send_real = total_down[0] * enter_real - total_down[1] * enter_imag + total_down[2]
        send_imag = total_down[0] * enter_imag + total_down[1] * enter_real + total_down[3]
        rise_real = total_up[0] * below_real - total_up[1] * below_imag + total_up[2]
        rise_imag = total_up[0] * below_imag + total_up[1] * below_real + total_up[3]
        got_down = from_behind((send_real, send_imag), "slab", 1)
        got_up = from_behind((rise_real, rise_imag), "slab", -1)
        return (got_down[0], got_down[1], got_up[0], got_up[1])

    enter_real, enter_imag, below_real, below_imag = lax.fori_loop(
        0, slab_count - 1, relay_turn, (zeros, zeros, zeros, zeros)
    )
    full_down_real = (
        local_down[:, :, 0]
        + down_real[:, None] * enter_real[None]
        - down_imag[:, None] * enter_imag[None]
    )
    full_down_imag = (
        local_down[:, :, 1]
        + down_real[:, None] * enter_imag[None]
        + down_imag[:, None] * enter_real[None]
    )
    full_up_real = (
        local_up[:, :, 0]
        + up_real[:, None] * below_real[None]
        - up_imag[:, None] * below_imag[None]
    )
    full_up_imag = (
        local_up[:, :, 1]
        + up_real[:, None] * below_imag[None]
        + up_imag[:, None] * below_real[None]
    )
    downward = jnp.stack([full_down_real, full_down_imag], axis=2)
    upward = jnp.stack([full_up_real, full_up_imag], axis=2)
    combined = (downward + upward - fields).reshape(layers, components, width_x, width_y)
    padded = padded_2(combined, (("px", 2), ("py", 3)), 1)
    neighbours = (
        padded[:, :, 2:, 1:-1]
        + padded[:, :, :-2, 1:-1]
        + padded[:, :, 1:-1, 2:]
        + padded[:, :, 1:-1, :-2]
    )
    return combined - 0.2 * (4.0 * combined - neighbours)


def solution(mesh):
    in_specs = (
        P("slab", None, "px", "py"),
        P("slab", "px", "py"),
        P("slab", "px", "py"),
        P("px", "py"),
        P("px", "py", None, "slab"),
        P("px", "py", "slab", None),
        P("px", "py", "slab"),
        P("px", "py", "slab"),
    )
    out_specs = P("slab", None, "px", "py")
    return jax.shard_map(shards, mesh=mesh, in_specs=in_specs, out_specs=out_specs, check_vma=False)
```

profile of v0, /device:TPU:0, one launch (start us, length us, event | category | flops | bytes accessed | tf_op | source)
XLA Modules:
  0.0 215.3 jit_solution(4807365809817015631)
XLA Ops:
  5.3 7.3 %all-to-all-start = ((s32[1,8,64]{2,0,1:T(1,128)}), s32[1,8,64]{2,0,1:T(1,128)S(1)}, u32[]{:S(2)}, u32[]{:S(2)}) async-start(s32[1,8,64]{2,0,1:T(1,128)} %reshape.138), calls=%async_computation | async-start | bytes 8192 | tf_op jit(solution)/shard_map/all_to_all | solution.py:67
  19.1 3.4 %all-to-all-start.1 = ((f32[8,1,256]{2,1,0:T(1,128)}), f32[8,1,256]{2,1,0:T(1,128)S(1)}, u32[]{:S(2)}, u32[]{:S(2)}) async-start(f32[8,1,256]{2,1,0:T(1,128)} %reshape.180), calls=%async_computation.1 | async-start | bytes 16384 | tf_op jit(solution)/shard_map/all_to_all | solution.py:60
  23.7 5.3 %all-to-all-done.1 = f32[8,1,256]{2,1,0:T(1,128)S(1)} async-done(((f32[8,1,256]{2,1,0:T(1,128)}), f32[8,1,256]{2,1,0:T(1,128)S(1)}, u32[]{:S(2)}, u32[]{:S(2)}) %all-to-all-start.1) | async-done | bytes 8224 | tf_op jit(solution)/shard_map/all_to_all | solution.py:60
  30.3 11.9 %scatter_fusion = f32[262144]{0:T(1024)S(1)} fusion(f32[262144]{0:T(1024)S(1)} %bitcast.140, s32[2048]{0:T(1024)S(1)} %bitcast.149, f32[2048]{0:T(1024)S(1)} %reshape.162), kind=kCustom, calls=%fused_computation.2 | custom fusion | flops 2048 | bytes 32768 | tf_op jit(solution)/shard_map/scatter-add | solution.py:79
  43.2 3.6 %while.65 = (s32[]{:T(128)}, f32[2,128,128]{2,1,0:T(8,128)S(1)}, f32[2,128,128]{2,1,0:T(8,128)S(1)}, f32[128,128]{1,0:T(8,128)S(1)}, f32[128,128]{1,0:T(8,128)S(...) while((s32[]{:T(128)}, f32[2,128,128]{2,1,0:T(8,128)S(1)}, ...), condition=%wide.region_9.10_spmd, body=%wide.region_8.9_spmd.sunk | while | flops 425987 | bytes 3014809 | solution.py:90
  49.3 3.5 %while.64 = (s32[]{:T(128)}, f32[2,128,128]{2,1,0:T(8,128)S(1)}, f32[2,128,128]{2,1,0:T(8,128)S(1)}, f32[128,128]{1,0:T(8,128)S(1)}, f32[128,128]{1,0:T(8,128)S(...) while((s32[]{:T(128)}, f32[2,128,128]{2,1,0:T(8,128)S(1)}, ...), condition=%wide.region_7.8_spmd, body=%wide.region_6.7_spmd.sunk | while | flops 425986 | bytes 3015297 | solution.py:89
  58.2 134.1 %while.66 = (s32[]{:T(128)}, f32[2,128,128]{2,1,0:T(8,128)S(1)}, f32[2,128,128]{2,1,0:T(8,128)S(1)}, f32[2,128,128]{2,1,0:T(8,128)S(1)}, f32[2,128,128]{2,1,0:T(...) while((s32[]{:T(128)}, f32[2,128,128]{2,1,0:T(8,128)S(1)}, ...), condition=%wide.region_11.12_spmd, body=%wide.region_10.11_spmd.sunk | while | flops 524290 | bytes 3932453 | solution.py:108
  61.6 3.3 %collective-permute-start.1 = (f32[2,128,128]{2,1,0:T(8,128)S(1)}, f32[2,128,128]{2,1,0:T(8,128)S(1)}, u32[]{:S(2)}, u32[]{:S(2)}) collective-permute-start(f32[2,128,128]{2,1,0:T(8,128)S(1)} %get-tuple-element.785), channel_id=1, source_target_pairs={{0,4},{4,8},{8,12},{12,16},{16,20},{20,24},{24,28},{1,5},{5,9},{9,... | collective-permute-start | bytes 393224 | tf_op jit(solution)/shard_map/while/body/eval_jaxpr/ppermute | solution.py:10
  69.1 4.4 %collective-permute-done.2 = f32[2,128,128]{2,1,0:T(8,128)S(1)} collective-permute-done((f32[2,128,128]{2,1,0:T(8,128)}, f32[2,128,128]{2,1,0:T(8,128)S(1)}, u32[]{:S(2)}, u32[]{:S(2)}) %collective-permute-start.2) | collective-permute-done | bytes 131104 | tf_op jit(solution)/shard_map/while/body/eval_jaxpr/ppermute | solution.py:10
  76.2 4.8 %collective-permute-start = (f32[2,128,128]{2,1,0:T(8,128)S(1)}, f32[2,128,128]{2,1,0:T(8,128)S(1)}, u32[]{:S(2)}, u32[]{:S(2)}) collective-permute-start(f32[2,128,128]{2,1,0:T(8,128)S(1)} %get-tuple-element.784), channel_id=1, source_target_pairs={{0,4},{4,8},{8,12},{12,16},{16,20},{20,24},{24,28},{1,5},{5,9},{9,... | collective-permute-start | bytes 393224 | tf_op jit(solution)/shard_map/while/body/eval_jaxpr/ppermute | solution.py:10
  87.7 4.4 %collective-permute-done.2 = f32[2,128,128]{2,1,0:T(8,128)S(1)} collective-permute-done((f32[2,128,128]{2,1,0:T(8,128)}, f32[2,128,128]{2,1,0:T(8,128)S(1)}, u32[]{:S(2)}, u32[]{:S(2)}) %collective-permute-start.2) | collective-permute-done | bytes 131104 | tf_op jit(solution)/shard_map/while/body/eval_jaxpr/ppermute | solution.py:10
  94.8 4.8 %collective-permute-start = (f32[2,128,128]{2,1,0:T(8,128)S(1)}, f32[2,128,128]{2,1,0:T(8,128)S(1)}, u32[]{:S(2)}, u32[]{:S(2)}) collective-permute-start(f32[2,128,128]{2,1,0:T(8,128)S(1)} %get-tuple-element.784), channel_id=1, source_target_pairs={{0,4},{4,8},{8,12},{12,16},{16,20},{20,24},{24,28},{1,5},{5,9},{9,... | collective-permute-start | bytes 393224 | tf_op jit(solution)/shard_map/while/body/eval_jaxpr/ppermute | solution.py:10
  107.2 4.4 %collective-permute-done.2 = f32[2,128,128]{2,1,0:T(8,128)S(1)} collective-permute-done((f32[2,128,128]{2,1,0:T(8,128)}, f32[2,128,128]{2,1,0:T(8,128)S(1)}, u32[]{:S(2)}, u32[]{:S(2)}) %collective-permute-start.2) | collective-permute-done | bytes 131104 | tf_op jit(solution)/shard_map/while/body/eval_jaxpr/ppermute | solution.py:10
  114.2 4.9 %collective-permute-start = (f32[2,128,128]{2,1,0:T(8,128)S(1)}, f32[2,128,128]{2,1,0:T(8,128)S(1)}, u32[]{:S(2)}, u32[]{:S(2)}) collective-permute-start(f32[2,128,128]{2,1,0:T(8,128)S(1)} %get-tuple-element.784), channel_id=1, source_target_pairs={{0,4},{4,8},{8,12},{12,16},{16,20},{20,24},{24,28},{1,5},{5,9},{9,... | collective-permute-start | bytes 393224 | tf_op jit(solution)/shard_map/while/body/eval_jaxpr/ppermute | solution.py:10
  126.0 4.2 %collective-permute-done.2 = f32[2,128,128]{2,1,0:T(8,128)S(1)} collective-permute-done((f32[2,128,128]{2,1,0:T(8,128)}, f32[2,128,128]{2,1,0:T(8,128)S(1)}, u32[]{:S(2)}, u32[]{:S(2)}) %collective-permute-start.2) | collective-permute-done | bytes 131104 | tf_op jit(solution)/shard_map/while/body/eval_jaxpr/ppermute | solution.py:10
  132.8 4.9 %collective-permute-start = (f32[2,128,128]{2,1,0:T(8,128)S(1)}, f32[2,128,128]{2,1,0:T(8,128)S(1)}, u32[]{:S(2)}, u32[]{:S(2)}) collective-permute-start(f32[2,128,128]{2,1,0:T(8,128)S(1)} %get-tuple-element.784), channel_id=1, source_target_pairs={{0,4},{4,8},{8,12},{12,16},{16,20},{20,24},{24,28},{1,5},{5,9},{9,... | collective-permute-start | bytes 393224 | tf_op jit(solution)/shard_map/while/body/eval_jaxpr/ppermute | solution.py:10
  145.2 4.4 %collective-permute-done.2 = f32[2,128,128]{2,1,0:T(8,128)S(1)} collective-permute-done((f32[2,128,128]{2,1,0:T(8,128)}, f32[2,128,128]{2,1,0:T(8,128)S(1)}, u32[]{:S(2)}, u32[]{:S(2)}) %collective-permute-start.2) | collective-permute-done | bytes 131104 | tf_op jit(solution)/shard_map/while/body/eval_jaxpr/ppermute | solution.py:10
  152.3 4.9 %collective-permute-start = (f32[2,128,128]{2,1,0:T(8,128)S(1)}, f32[2,128,128]{2,1,0:T(8,128)S(1)}, u32[]{:S(2)}, u32[]{:S(2)}) collective-permute-start(f32[2,128,128]{2,1,0:T(8,128)S(1)} %get-tuple-element.784), channel_id=1, source_target_pairs={{0,4},{4,8},{8,12},{12,16},{16,20},{20,24},{24,28},{1,5},{5,9},{9,... | collective-permute-start | bytes 393224 | tf_op jit(solution)/shard_map/while/body/eval_jaxpr/ppermute | solution.py:10
  157.2 3.9 %collective-permute-start.1 = (f32[2,128,128]{2,1,0:T(8,128)S(1)}, f32[2,128,128]{2,1,0:T(8,128)S(1)}, u32[]{:S(2)}, u32[]{:S(2)}) collective-permute-start(f32[2,128,128]{2,1,0:T(8,128)S(1)} %get-tuple-element.785), channel_id=1, source_target_pairs={{0,4},{4,8},{8,12},{12,16},{16,20},{20,24},{24,28},{1,5},{5,9},{9,... | collective-permute-start | bytes 393224 | tf_op jit(solution)/shard_map/while/body/eval_jaxpr/ppermute | solution.py:10
  165.3 4.4 %collective-permute-done.2 = f32[2,128,128]{2,1,0:T(8,128)S(1)} collective-permute-done((f32[2,128,128]{2,1,0:T(8,128)}, f32[2,128,128]{2,1,0:T(8,128)S(1)}, u32[]{:S(2)}, u32[]{:S(2)}) %collective-permute-start.2) | collective-permute-done | bytes 131104 | tf_op jit(solution)/shard_map/while/body/eval_jaxpr/ppermute | solution.py:10
  172.3 4.8 %collective-permute-start = (f32[2,128,128]{2,1,0:T(8,128)S(1)}, f32[2,128,128]{2,1,0:T(8,128)S(1)}, u32[]{:S(2)}, u32[]{:S(2)}) collective-permute-start(f32[2,128,128]{2,1,0:T(8,128)S(1)} %get-tuple-element.784), channel_id=1, source_target_pairs={{0,4},{4,8},{8,12},{12,16},{16,20},{20,24},{24,28},{1,5},{5,9},{9,... | collective-permute-start | bytes 393224 | tf_op jit(solution)/shard_map/while/body/eval_jaxpr/ppermute | solution.py:10
  177.2 4.7 %collective-permute-start.1 = (f32[2,128,128]{2,1,0:T(8,128)S(1)}, f32[2,128,128]{2,1,0:T(8,128)S(1)}, u32[]{:S(2)}, u32[]{:S(2)}) collective-permute-start(f32[2,128,128]{2,1,0:T(8,128)S(1)} %get-tuple-element.785), channel_id=1, source_target_pairs={{0,4},{4,8},{8,12},{12,16},{16,20},{20,24},{24,28},{1,5},{5,9},{9,... | collective-permute-start | bytes 393224 | tf_op jit(solution)/shard_map/while/body/eval_jaxpr/ppermute | solution.py:10
  186.1 4.4 %collective-permute-done.2 = f32[2,128,128]{2,1,0:T(8,128)S(1)} collective-permute-done((f32[2,128,128]{2,1,0:T(8,128)}, f32[2,128,128]{2,1,0:T(8,128)S(1)}, u32[]{:S(2)}, u32[]{:S(2)}) %collective-permute-start.2) | collective-permute-done | bytes 131104 | tf_op jit(solution)/shard_map/while/body/eval_jaxpr/ppermute | solution.py:10
  195.7 4.5 %collective-permute-start.5 = (f32[4,4,1,128]{3,2,1,0:T(1,128)S(1)}, f32[4,4,1,128]{3,2,1,0:T(1,128)S(1)}, u32[]{:S(2)}, u32[]{:S(2)}) collective-permute-start(f32[4,4,1,128]{3,2,1,0:T(1,128)S(1)} %get-tuple-element.525), channel_id=1, source_target_pairs={{0,2},{1,3},{4,6},{5,7},{8,10},{9,11},{12,14},{13,15},{16,18},{17,... | collective-permute-start | bytes 24584 | tf_op jit(solution)/shard_map/ppermute | solution.py:18
  (204 shorter events, 109.6 us)
Async XLA Ops:
  5.3 13.7 %all-to-all-start = ((s32[1,8,64]{2,0,1:T(1,128)}), s32[1,8,64]{2,0,1:T(1,128)S(1)}, u32[]{:S(2)}, u32[]{:S(2)}) async-start(s32[1,8,64]{2,0,1:T(1,128)} %reshape.138), calls=%async_computation | async-start | bytes 8192 | tf_op jit(solution)/shard_map/all_to_all | solution.py:67
  19.1 9.9 %all-to-all-start.1 = ((f32[8,1,256]{2,1,0:T(1,128)}), f32[8,1,256]{2,1,0:T(1,128)S(1)}, u32[]{:S(2)}, u32[]{:S(2)}) async-start(f32[8,1,256]{2,1,0:T(1,128)} %reshape.180), calls=%async_computation.1 | async-start | bytes 16384 | tf_op jit(solution)/shard_map/all_to_all | solution.py:60
  59.1 10.0 %collective-permute-start = (f32[2,128,128]{2,1,0:T(8,128)S(1)}, f32[2,128,128]{2,1,0:T(8,128)S(1)}, u32[]{:S(2)}, u32[]{:S(2)}) collective-permute-start(f32[2,128,128]{2,1,0:T(8,128)S(1)} %get-tuple-element.784), channel_id=1, source_target_pairs={{0,4},{4,8},{8,12},{12,16},{16,20},{20,24},{24,28},{1,5},{5,9},{9,... | collective-permute-start | bytes 393224 | tf_op jit(solution)/shard_map/while/body/eval_jaxpr/ppermute | solution.py:10
  61.6 7.5 %collective-permute-start.1 = (f32[2,128,128]{2,1,0:T(8,128)S(1)}, f32[2,128,128]{2,1,0:T(8,128)S(1)}, u32[]{:S(2)}, u32[]{:S(2)}) collective-permute-start(f32[2,128,128]{2,1,0:T(8,128)S(1)} %get-tuple-element.785), channel_id=1, source_target_pairs={{0,4},{4,8},{8,12},{12,16},{16,20},{20,24},{24,28},{1,5},{5,9},{9,... | collective-permute-start | bytes 393224 | tf_op jit(solution)/shard_map/while/body/eval_jaxpr/ppermute | solution.py:10
  66.5 7.1 %collective-permute-start.2 = (f32[2,128,128]{2,1,0:T(8,128)}, f32[2,128,128]{2,1,0:T(8,128)S(1)}, u32[]{:S(2)}, u32[]{:S(2)}) collective-permute-start(f32[2,128,128]{2,1,0:T(8,128)} %get-tuple-element.786), channel_id=1, source_target_pairs={{4,0},{8,4},{12,8},{16,12},{20,16},{24,20},{28,24},{5,1},{9,5},{13... | collective-permute-start | bytes 393224 | tf_op jit(solution)/shard_map/while/body/eval_jaxpr/ppermute | solution.py:10
  67.8 7.5 %collective-permute-start.3 = (f32[2,128,128]{2,1,0:T(8,128)S(1)}, f32[2,128,128]{2,1,0:T(8,128)S(1)}, u32[]{:S(2)}, u32[]{:S(2)}) collective-permute-start(f32[2,128,128]{2,1,0:T(8,128)S(1)} %get-tuple-element.787), channel_id=1, source_target_pairs={{4,0},{8,4},{12,8},{16,12},{20,16},{24,20},{28,24},{5,1},{9,5},{13... | collective-permute-start | bytes 393224 | tf_op jit(solution)/shard_map/while/body/eval_jaxpr/ppermute | solution.py:10
  76.2 11.5 %collective-permute-start = (f32[2,128,128]{2,1,0:T(8,128)S(1)}, f32[2,128,128]{2,1,0:T(8,128)S(1)}, u32[]{:S(2)}, u32[]{:S(2)}) collective-permute-start(f32[2,128,128]{2,1,0:T(8,128)S(1)} %get-tuple-element.784), channel_id=1, source_target_pairs={{0,4},{4,8},{8,12},{12,16},{16,20},{20,24},{24,28},{1,5},{5,9},{9,... | collective-permute-start | bytes 393224 | tf_op jit(solution)/shard_map/while/body/eval_jaxpr/ppermute | solution.py:10
  86.4 7.5 %collective-permute-start.3 = (f32[2,128,128]{2,1,0:T(8,128)S(1)}, f32[2,128,128]{2,1,0:T(8,128)S(1)}, u32[]{:S(2)}, u32[]{:S(2)}) collective-permute-start(f32[2,128,128]{2,1,0:T(8,128)S(1)} %get-tuple-element.787), channel_id=1, source_target_pairs={{4,0},{8,4},{12,8},{16,12},{20,16},{24,20},{28,24},{5,1},{9,5},{13... | collective-permute-start | bytes 393224 | tf_op jit(solution)/shard_map/while/body/eval_jaxpr/ppermute | solution.py:10
  94.8 12.3 %collective-permute-start = (f32[2,128,128]{2,1,0:T(8,128)S(1)}, f32[2,128,128]{2,1,0:T(8,128)S(1)}, u32[]{:S(2)}, u32[]{:S(2)}) collective-permute-start(f32[2,128,128]{2,1,0:T(8,128)S(1)} %get-tuple-element.784), channel_id=1, source_target_pairs={{0,4},{4,8},{8,12},{12,16},{16,20},{20,24},{24,28},{1,5},{5,9},{9,... | collective-permute-start | bytes 393224 | tf_op jit(solution)/shard_map/while/body/eval_jaxpr/ppermute | solution.py:10
  99.6 7.5 %collective-permute-start.1 = (f32[2,128,128]{2,1,0:T(8,128)S(1)}, f32[2,128,128]{2,1,0:T(8,128)S(1)}, u32[]{:S(2)}, u32[]{:S(2)}) collective-permute-start(f32[2,128,128]{2,1,0:T(8,128)S(1)} %get-tuple-element.785), channel_id=1, source_target_pairs={{0,4},{4,8},{8,12},{12,16},{16,20},{20,24},{24,28},{1,5},{5,9},{9,... | collective-permute-start | bytes 393224 | tf_op jit(solution)/shard_map/while/body/eval_jaxpr/ppermute | solution.py:10
  104.5 7.1 %collective-permute-start.2 = (f32[2,128,128]{2,1,0:T(8,128)}, f32[2,128,128]{2,1,0:T(8,128)S(1)}, u32[]{:S(2)}, u32[]{:S(2)}) collective-permute-start(f32[2,128,128]{2,1,0:T(8,128)} %get-tuple-element.786), channel_id=1, source_target_pairs={{4,0},{8,4},{12,8},{16,12},{20,16},{24,20},{28,24},{5,1},{9,5},{13... | collective-permute-start | bytes 393224 | tf_op jit(solution)/shard_map/while/body/eval_jaxpr/ppermute | solution.py:10
  105.8 7.5 %collective-permute-start.3 = (f32[2,128,128]{2,1,0:T(8,128)S(1)}, f32[2,128,128]{2,1,0:T(8,128)S(1)}, u32[]{:S(2)}, u32[]{:S(2)}) collective-permute-start(f32[2,128,128]{2,1,0:T(8,128)S(1)} %get-tuple-element.787), channel_id=1, source_target_pairs={{4,0},{8,4},{12,8},{16,12},{20,16},{24,20},{28,24},{5,1},{9,5},{13... | collective-permute-start | bytes 393224 | tf_op jit(solution)/shard_map/while/body/eval_jaxpr/ppermute | solution.py:10
  114.2 11.4 %collective-permute-start = (f32[2,128,128]{2,1,0:T(8,128)S(1)}, f32[2,128,128]{2,1,0:T(8,128)S(1)}, u32[]{:S(2)}, u32[]{:S(2)}) collective-permute-start(f32[2,128,128]{2,1,0:T(8,128)S(1)} %get-tuple-element.784), channel_id=1, source_target_pairs={{0,4},{4,8},{8,12},{12,16},{16,20},{20,24},{24,28},{1,5},{5,9},{9,... | collective-permute-start | bytes 393224 | tf_op jit(solution)/shard_map/while/body/eval_jaxpr/ppermute | solution.py:10
  123.1 7.1 %collective-permute-start.2 = (f32[2,128,128]{2,1,0:T(8,128)}, f32[2,128,128]{2,1,0:T(8,128)S(1)}, u32[]{:S(2)}, u32[]{:S(2)}) collective-permute-start(f32[2,128,128]{2,1,0:T(8,128)} %get-tuple-element.786), channel_id=1, source_target_pairs={{4,0},{8,4},{12,8},{16,12},{20,16},{24,20},{28,24},{5,1},{9,5},{13... | collective-permute-start | bytes 393224 | tf_op jit(solution)/shard_map/while/body/eval_jaxpr/ppermute | solution.py:10
  124.4 7.5 %collective-permute-start.3 = (f32[2,128,128]{2,1,0:T(8,128)S(1)}, f32[2,128,128]{2,1,0:T(8,128)S(1)}, u32[]{:S(2)}, u32[]{:S(2)}) collective-permute-start(f32[2,128,128]{2,1,0:T(8,128)S(1)} %get-tuple-element.787), channel_id=1, source_target_pairs={{4,0},{8,4},{12,8},{16,12},{20,16},{24,20},{28,24},{5,1},{9,5},{13... | collective-permute-start | bytes 393224 | tf_op jit(solution)/shard_map/while/body/eval_jaxpr/ppermute | solution.py:10
  132.8 12.4 %collective-permute-start = (f32[2,128,128]{2,1,0:T(8,128)S(1)}, f32[2,128,128]{2,1,0:T(8,128)S(1)}, u32[]{:S(2)}, u32[]{:S(2)}) collective-permute-start(f32[2,128,128]{2,1,0:T(8,128)S(1)} %get-tuple-element.784), channel_id=1, source_target_pairs={{0,4},{4,8},{8,12},{12,16},{16,20},{20,24},{24,28},{1,5},{5,9},{9,... | collective-permute-start | bytes 393224 | tf_op jit(solution)/shard_map/while/body/eval_jaxpr/ppermute | solution.py:10
  137.7 7.5 %collective-permute-start.1 = (f32[2,128,128]{2,1,0:T(8,128)S(1)}, f32[2,128,128]{2,1,0:T(8,128)S(1)}, u32[]{:S(2)}, u32[]{:S(2)}) collective-permute-start(f32[2,128,128]{2,1,0:T(8,128)S(1)} %get-tuple-element.785), channel_id=1, source_target_pairs={{0,4},{4,8},{8,12},{12,16},{16,20},{20,24},{24,28},{1,5},{5,9},{9,... | collective-permute-start | bytes 393224 | tf_op jit(solution)/shard_map/while/body/eval_jaxpr/ppermute | solution.py:10
  143.8 7.5 %collective-permute-start.3 = (f32[2,128,128]{2,1,0:T(8,128)S(1)}, f32[2,128,128]{2,1,0:T(8,128)S(1)}, u32[]{:S(2)}, u32[]{:S(2)}) collective-permute-start(f32[2,128,128]{2,1,0:T(8,128)S(1)} %get-tuple-element.787), channel_id=1, source_target_pairs={{4,0},{8,4},{12,8},{16,12},{20,16},{24,20},{28,24},{5,1},{9,5},{13... | collective-permute-start | bytes 393224 | tf_op jit(solution)/shard_map/while/body/eval_jaxpr/ppermute | solution.py:10
  152.3 13.0 %collective-permute-start = (f32[2,128,128]{2,1,0:T(8,128)S(1)}, f32[2,128,128]{2,1,0:T(8,128)S(1)}, u32[]{:S(2)}, u32[]{:S(2)}) collective-permute-start(f32[2,128,128]{2,1,0:T(8,128)S(1)} %get-tuple-element.784), channel_id=1, source_target_pairs={{0,4},{4,8},{8,12},{12,16},{16,20},{20,24},{24,28},{1,5},{5,9},{9,... | collective-permute-start | bytes 393224 | tf_op jit(solution)/shard_map/while/body/eval_jaxpr/ppermute | solution.py:10
  157.2 8.1 %collective-permute-start.1 = (f32[2,128,128]{2,1,0:T(8,128)S(1)}, f32[2,128,128]{2,1,0:T(8,128)S(1)}, u32[]{:S(2)}, u32[]{:S(2)}) collective-permute-start(f32[2,128,128]{2,1,0:T(8,128)S(1)} %get-tuple-element.785), channel_id=1, source_target_pairs={{0,4},{4,8},{8,12},{12,16},{16,20},{20,24},{24,28},{1,5},{5,9},{9,... | collective-permute-start | bytes 393224 | tf_op jit(solution)/shard_map/while/body/eval_jaxpr/ppermute | solution.py:10
  163.9 7.5 %collective-permute-start.3 = (f32[2,128,128]{2,1,0:T(8,128)S(1)}, f32[2,128,128]{2,1,0:T(8,128)S(1)}, u32[]{:S(2)}, u32[]{:S(2)}) collective-permute-start(f32[2,128,128]{2,1,0:T(8,128)S(1)} %get-tuple-element.787), channel_id=1, source_target_pairs={{4,0},{8,4},{12,8},{16,12},{20,16},{24,20},{28,24},{5,1},{9,5},{13... | collective-permute-start | bytes 393224 | tf_op jit(solution)/shard_map/while/body/eval_jaxpr/ppermute | solution.py:10
  172.3 13.7 %collective-permute-start = (f32[2,128,128]{2,1,0:T(8,128)S(1)}, f32[2,128,128]{2,1,0:T(8,128)S(1)}, u32[]{:S(2)}, u32[]{:S(2)}) collective-permute-start(f32[2,128,128]{2,1,0:T(8,128)S(1)} %get-tuple-element.784), channel_id=1, source_target_pairs={{0,4},{4,8},{8,12},{12,16},{16,20},{20,24},{24,28},{1,5},{5,9},{9,... | collective-permute-start | bytes 393224 | tf_op jit(solution)/shard_map/while/body/eval_jaxpr/ppermute | solution.py:10
  177.2 8.9 %collective-permute-start.1 = (f32[2,128,128]{2,1,0:T(8,128)S(1)}, f32[2,128,128]{2,1,0:T(8,128)S(1)}, u32[]{:S(2)}, u32[]{:S(2)}) collective-permute-start(f32[2,128,128]{2,1,0:T(8,128)S(1)} %get-tuple-element.785), channel_id=1, source_target_pairs={{0,4},{4,8},{8,12},{12,16},{16,20},{20,24},{24,28},{1,5},{5,9},{9,... | collective-permute-start | bytes 393224 | tf_op jit(solution)/shard_map/while/body/eval_jaxpr/ppermute | solution.py:10
  184.8 7.5 %collective-permute-start.3 = (f32[2,128,128]{2,1,0:T(8,128)S(1)}, f32[2,128,128]{2,1,0:T(8,128)S(1)}, u32[]{:S(2)}, u32[]{:S(2)}) collective-permute-start(f32[2,128,128]{2,1,0:T(8,128)S(1)} %get-tuple-element.787), channel_id=1, source_target_pairs={{4,0},{8,4},{12,8},{16,12},{20,16},{24,20},{28,24},{5,1},{9,5},{13... | collective-permute-start | bytes 393224 | tf_op jit(solution)/shard_map/while/body/eval_jaxpr/ppermute | solution.py:10
  (24 other events, 152.8 us)
where the time goes:
time: 218 us; the launch traced here: 215 us
  starting transfers between devices  94 us (43%)
  waiting for transfers between devices  52.8 us (24%)
  other arithmetic  44.6 us (20%)
  local copies, waits for them, and re-layouts  22.7 us (10%)
    ppermute x28, starting transfers between devices, from_behind(): return lax.ppermute(array, axis, pairs)  73.2 us
    ppermute x28, waiting for transfers between devices, from_behind(): return lax.ppermute(array, axis, pairs)  43.2 us
    scatter-add x1, other arithmetic, shards(): forcing = source.reshape(-1).at[flat_index].add(inject_values.reshape(-1))  11.9 us
    add x7, other arithmetic, relay_turn(): total_up[0] * below_imag + total_up[1] * below_real + total_up[3]  10.9 us
    ppermute x2, starting transfers between devices, padded_2(): lax.ppermute(lax.slice_in_dim(block, block.shape[dim] - width, None, axis...  7.57 us
    all_to_all x1, starting transfers between devices, shards(): lax.all_to_all(send_places.reshape(1, slab_count, capacity), 'slab', spli...  7.28 us
    add x7, other arithmetic, relay_turn(): total_down[0] * enter_imag + total_down[1] * enter_real + total_down[3]  6.37 us
    dynamic_update_slice x24, other arithmetic, shards(): lax.scan(advance, start_state, (real_mult, imag_mult, fields))  5.8 us
  transfers between devices with their start and end apart: 34, of which 19 were waited for; matrix products, arithmetic and copies ran while one was open for 8% of the time, Pallas kernels for 0%

commit v1 on v0

v1 whole, which is shorter than its diff:
```python
import functools

import jax
import jax.numpy as jnp
from jax import lax
from jax.experimental import pallas as pl
from jax.experimental.pallas import tpu as pltpu
from jax.sharding import PartitionSpec as P

CHUNKS = 4
LANES = 128
CAP = 64
BF16 = jnp.bfloat16
F32 = jnp.float32


def thirds(value):
    high = value.astype(BF16)
    rest = value - high.astype(F32)
    mid = rest.astype(BF16)
    low = (rest - mid.astype(F32)).astype(BF16)
    return high, mid, low


def times(rate, state):
    return rate[0] * state[0] - rate[1] * state[1], rate[0] * state[1] + rate[1] * state[0]


def kernel(
    sizes,
    src_hbm, phase_hbm, att_hbm, pml_hbm, vals, rslab, rlat, rlay,
    out,
    force, phase, att, pml, rate_re, rate_im,
    data, spread, arrived, left, right,
    prod_send, prod_pair, fwd_send, pair,
    down_send, down_recv, up_send, up_recv,
    down_back, up_back, enter_down, enter_up,
    comb, row_send, row_recv, col_send, col_recv,
    in_sem, spread_s, spread_r, prod_s, prod_r, fwd_s, fwd_r,
    down_s, down_r, up_s, up_r, dback_s, dback_r, uback_s, uback_r,
    row_s, row_r, col_s, col_r,
):
    S, L, C, X, Y, K = sizes
    G = S // 2
    H = X // 2
    R = H // K
    shots = C // 2
    me = lax.axis_index("slab")
    px = lax.axis_index("px")
    py = lax.axis_index("py")
    g = lax.div(me, 2)
    y = lax.rem(me, 2)
    partner = {"slab": g * 2 + (1 - y)}
    other_x = {"px": 1 - px}
    other_y = {"py": 1 - py}

    def remote(src, dst, send, recv, where):
        return pltpu.make_async_remote_copy(
            src_ref=src, dst_ref=dst, send_sem=send, recv_sem=recv,
            device_id=where, device_id_type=pl.DeviceIdType.MESH,
        )

    barrier = pltpu.get_barrier_semaphore()
    peers = [lax.rem(me + step, S) for step in range(1, S)]
    for where in [{"slab": peer} for peer in peers] + [other_x, other_y]:
        pl.semaphore_signal(barrier, inc=1, device_id=where, device_id_type=pl.DeviceIdType.MESH)

    loads = [
        pltpu.make_async_copy(a, b, in_sem.at[i])
        for i, (a, b) in enumerate(
            ((phase_hbm, phase), (att_hbm, att), (pml_hbm, pml), (src_hbm, force))
        )
    ]
    for load in loads:
        load.start()

    rows = vals.shape[1]
    lane = lax.broadcasted_iota(jnp.int32, (rows, LANES), 1)
    slab_of = rslab[...]
    hot = jnp.where(lane == slab_of, 1.0, 0.0)
    earlier = jnp.where(
        lax.broadcasted_iota(jnp.int32, (rows, rows), 1)
        < lax.broadcasted_iota(jnp.int32, (rows, rows), 0),
        1.0, 0.0,
    ).astype(BF16)
    before = jnp.dot(earlier, hot.astype(BF16), preferred_element_type=F32)
    rank = jnp.sum(before * hot, axis=1, keepdims=True).astype(jnp.int32)
    slot = slab_of * LANES + rank
    place = jnp.where(
        lax.broadcasted_iota(jnp.int32, (rows, S * LANES), 1) == slot, 1.0, 0.0
    ).astype(BF16)
    lateral = rlat[...]
    data[...] = jnp.zeros_like(data)
    data[0:C, :] = vals[...]
    data[C : C + 1, :] = (rlay[...] * X + lax.div(lateral, Y)).astype(F32)
    data[C + 1 : C + 2, :] = lax.rem(lateral, Y).astype(F32)
    routed = sum(
        jnp.dot(part, place, preferred_element_type=F32) for part in thirds(data[...])
    )
    for s in range(S):
        spread[s] = routed[:, s * LANES : (s + 1) * LANES]

    pl.semaphore_wait(barrier, S + 1)
    arrived[me] = spread[me]
    spreads = []
    for peer in peers:
        copy = remote(
            spread.at[peer], arrived.at[me], spread_s.at[peer], spread_r.at[me], {"slab": peer}
        )
        copy.start()
        spreads.append(copy)

    for load in loads[:3]:
        load.wait()
    for l in range(L):
        damping = att[l] + (0.5 / (L * S)) * pml[...].astype(F32)
        amplitude = jnp.exp(-damping)
        rate_re[l] = amplitude * jnp.cos(phase[l])
        rate_im[l] = amplitude * jnp.sin(phase[l])

    def product(half):
        at = pl.ds(pl.multiple_of(half * H, H), H)
        total = (rate_re[0, at], rate_im[0, at])
        for l in range(1, L):
            total = times((rate_re[l, at], rate_im[l, at]), total)
        return total

    total = product(1 - y)
    prod_send[0] = total[0]
    prod_send[1] = total[1]
    send_prod = remote(prod_send, prod_pair.at[y], prod_s, prod_r, partner)
    send_prod.start()
    total = product(y)
    prod_pair[y, 0] = total[0]
    prod_pair[y, 1] = total[1]

    loads[3].wait()
    for peer in peers:
        remote(
            spread.at[peer], arrived.at[peer], spread_s.at[peer], spread_r.at[peer], {"slab": peer}
        ).wait_recv()
    slots = S * CAP
    got = jnp.concatenate(
        [arrived[2 * i] + pltpu.roll(arrived[2 * i + 1], CAP, 1) for i in range(S // 2)], axis=1
    )
    row_at = got[C : C + 1, :].astype(jnp.int32)
    col_at = got[C + 1 : C + 2, :].astype(jnp.int32)
    on_row = jnp.where(
        lax.broadcasted_iota(jnp.int32, (L * X, slots), 0) == row_at, 1.0, 0.0
    ).astype(BF16)
    on_col = lax.broadcasted_iota(jnp.int32, (Y, slots), 0) == col_at
    parts = thirds(got)
    for i in range(3):
        left[:, i * slots : (i + 1) * slots] = on_row
        part = parts[i].astype(F32)
        for c in range(C):
            right[c * Y : (c + 1) * Y, i * slots : (i + 1) * slots] = jnp.where(
                on_col, part[c : c + 1, :], 0.0
            ).astype(BF16)
    for l in range(L):
        added = lax.dot_general(
            left[l * X : (l + 1) * X, :], right[...], (((1,), (1,)), ((), ())),
            preferred_element_type=F32,
        )
        for c in range(C):
            force[l, c] += added[:, c * Y : (c + 1) * Y]

    def local(half, k, dst):
        at = pl.ds(pl.multiple_of(half * H + k * R, R), R)
        rates = [(rate_re[l, at], rate_im[l, at]) for l in range(L)]
        for s in range(shots):
            f = [(force[l, 2 * s, at], force[l, 2 * s + 1, at]) for l in range(L)]
            w = f[0]
            for l in range(1, L):
                re, im = times(rates[l], w)
                w = (re + f[l][0], im + f[l][1])
            v = f[L - 1]
            for l in range(L - 2, -1, -1):
                re, im = times(rates[l], v)
                v = (re + f[l][0], im + f[l][1])
            dst[2 * s] = w[0]
            dst[2 * s + 1] = w[1]
            dst[C + 2 * s] = v[0]
            dst[C + 2 * s + 1] = v[1]

    sends = []
    for k in range(K):
        local(1 - y, k, fwd_send.at[k])
        copy = remote(fwd_send.at[k], pair.at[y, k], fwd_s.at[k], fwd_r.at[k], partner)
        copy.start()
        sends.append(copy)
    for k in range(K):
        local(y, k, pair.at[y, k])

    @pl.when(g == 0)
    def _():
        down_recv[...] = jnp.zeros_like(down_recv)

    @pl.when(g == G - 1)
    def _():
        up_recv[...] = jnp.zeros_like(up_recv)

    def down_copy(k):
        return remote(down_send.at[k], down_recv.at[k], down_s.at[k], down_r.at[k], {"slab": me + 2})

    def up_copy(k):
        return remote(up_send.at[k], up_recv.at[k], up_s.at[k], up_r.at[k], {"slab": me - 2})

    def down_back_copy(k):
        return remote(down_back.at[k], enter_down.at[y, k], dback_s.at[k], dback_r.at[k], partner)

    def up_back_copy(k):
        return remote(up_back.at[k], enter_up.at[y, k], uback_s.at[k], uback_r.at[k], partner)

    def factors(k, member):
        at = pl.ds(pl.multiple_of(k * R, R), R)
        return prod_pair[member, 0, at], prod_pair[member, 1, at]

    def hop(k, first, second, base, incoming, outgoing, own, theirs, own_direct):
        near, far = factors(k, first), factors(k, second)
        for s in range(shots):
            i, j = 2 * s, 2 * s + 1
            e = (incoming[k, i], incoming[k, j])
            re, im = times(near, e)
            q = (re + pair[first, k, base + i], im + pair[first, k, base + j])
            re, im = times(far, q)
            outgoing[k, i] = re + pair[second, k, base + i]
            outgoing[k, j] = im + pair[second, k, base + j]
            for a in (0, 1):
                own[y, k, 2 * s + a] = jnp.where(own_direct, e[a], q[a])
                theirs[k, 2 * s + a] = jnp.where(own_direct, q[a], e[a])

    send_prod.wait_recv()
    for t in range(K + G - 1):
        if t < K:
            remote(
                fwd_send.at[t], pair.at[1 - y, t], fwd_s.at[t], fwd_r.at[t], partner
            ).wait_recv()
        kd = t - g
        ku = t - (G - 1 - g)

        @pl.when((kd >= 0) & (kd < K))
        def _():
            @pl.when(g > 0)
            def _():
                remote(
                    down_send.at[kd], down_recv.at[kd], down_s.at[kd], down_r.at[kd], {"slab": me - 2}
                ).wait_recv()

            hop(kd, 0, 1, 0, down_recv, down_send, enter_down, down_back, y == 0)

            @pl.when(g < G - 1)
            def _():
                down_copy(kd).start()

            down_back_copy(kd).start()

        @pl.when((ku >= 0) & (ku < K))
        def _():
            @pl.when(g < G - 1)
            def _():
                remote(
                    up_send.at[ku], up_recv.at[ku], up_s.at[ku], up_r.at[ku], {"slab": me + 2}
                ).wait_recv()

            hop(ku, 1, 0, C, up_recv, up_send, enter_up, up_back, y == 1)

            @pl.when(g > 0)
            def _():
                up_copy(ku).start()

            up_back_copy(ku).start()

    pad = comb.shape[2] // 2 - X // 2

    def full(half, k):
        row = half * H + k * R
        at = pl.ds(pl.multiple_of(row, R), R)
        to = pl.ds(pl.multiple_of(row + pad, 8), R)
        rates = [(rate_re[l, at], rate_im[l, at]) for l in range(L)]
        for s in range(shots):
            i, j = 2 * s, 2 * s + 1
            f = [(force[l, i, at], force[l, j, at]) for l in range(L)]
            w = (enter_down[half, k, i], enter_down[half, k, j])
            downs = []
            for l in range(L):
                re, im = times(rates[l], w)
                w = (re + f[l][0], im + f[l][1])
                downs.append(w)
            v = (enter_up[half, k, i], enter_up[half, k, j])
            for l in range(L - 1, -1, -1):
                re, im = times(rates[l], v)
                comb[l, i, to] = downs[l][0] + re
                comb[l, j, to] = downs[l][1] + im
                v = (re + f[l][0], im + f[l][1])

    for k in range(K):
        full(y, k)
    for k in range(K):
        remote(
            down_back.at[k], enter_down.at[1 - y, k], dback_s.at[k], dback_r.at[k], partner
        ).wait_recv()
        remote(
            up_back.at[k], enter_up.at[1 - y, k], uback_s.at[k], uback_r.at[k], partner
        ).wait_recv()
        full(1 - y, k)

    edge_lane = lax.broadcasted_iota(jnp.int32, (X, LANES), 1)

    def send_rows(row):
        for l in range(L):
            for c in range(C):
                row_send[l * C + c : l * C + c + 1, :] = comb[l, c, pad + row : pad + row + 1, :]

    def send_cols(col):
        held = jnp.zeros((X, LANES), F32)
        for l in range(L):
            for c in range(C):
                column = comb[l, c, pad : pad + X, col : col + 1]
                held = jnp.where(edge_lane == l * C + c, column, held)
        col_send[...] = held

    pl.when(px == 0)(lambda: send_rows(X - 1))
    pl.when(px == 1)(lambda: send_rows(0))
    rows_out = remote(row_send, row_recv, row_s, row_r, other_x)
    rows_out.start()
    pl.when(py == 0)(lambda: send_cols(Y - 1))
    pl.when(py == 1)(lambda: send_cols(0))
    cols_out = remote(col_send, col_recv, col_s, col_r, other_y)
    cols_out.start()

    full_lane = lax.broadcasted_iota(jnp.int32, (X, Y), 1)
    for l in range(L):
        for c in range(C):
            comb[l, c, pad - 1 : pad, :] = jnp.zeros((1, Y), F32)
            comb[l, c, pad + X : pad + X + 1, :] = jnp.zeros((1, Y), F32)
            here = comb[l, c, pad : pad + X, :]
            around = comb[l, c, pad - 1 : pad - 1 + X, :] + comb[l, c, pad + 1 : pad + 1 + X, :]
            around += jnp.where(full_lane == 0, 0.0, pltpu.roll(here, 1, 1))
            around += jnp.where(full_lane == Y - 1, 0.0, pltpu.roll(here, Y - 1, 1))
            out[l, c] = here - 0.2 * (4.0 * here - around)

    rows_out.wait_recv()

    def add_rows(row):
        for l in range(L):
            for c in range(C):
                out[l, c, row : row + 1, :] += 0.2 * row_recv[l * C + c : l * C + c + 1, :]

    pl.when(px == 0)(lambda: add_rows(X - 1))
    pl.when(px == 1)(lambda: add_rows(0))
    cols_out.wait_recv()
    at_edge = full_lane == jnp.where(py == 0, Y - 1, 0)
    for l in range(L):
        for c in range(C):
            i = l * C + c
            out[l, c] += jnp.where(at_edge, 0.2 * col_recv[:, i : i + 1], 0.0)

    for copy in spreads + sends + [send_prod, rows_out, cols_out]:
        copy.wait_send()
    for k in range(K):
        down_back_copy(k).wait_send()
        up_back_copy(k).wait_send()

    @pl.when(g < G - 1)
    def _():
        for k in range(K):
            down_copy(k).wait_send()

    @pl.when(g > 0)
    def _():
        for k in range(K):
            up_copy(k).wait_send()


def shards(source, phase, attenuation, pml_level, recv_values, recv_slab, recv_lateral, recv_layer):
    L, C, X, Y = source.shape
    S = lax.axis_size("slab")
    rows = recv_values.shape[3]
    K = CHUNKS
    H = X // 2
    R = H // K
    vmem, dma = pltpu.VMEM, pltpu.SemaphoreType.DMA
    chunked = vmem((K, C, R, Y), F32)
    scratch = [
        vmem((L, C, X, Y), F32), vmem((L, X, Y), F32), vmem((L, X, Y), F32), vmem((X, Y), jnp.int32),
        vmem((L, X, Y), F32), vmem((L, X, Y), F32),
        vmem((8, rows), F32), vmem((S, 8, LANES), F32), vmem((S, 8, LANES), F32),
        vmem((L * X, 3 * S * CAP), BF16), vmem((C * Y, 3 * S * CAP), BF16),
        vmem((2, H, Y), F32), vmem((2, 2, H, Y), F32),
        vmem((K, 2 * C, R, Y), F32), vmem((2, K, 2 * C, R, Y), F32),
        chunked, chunked, chunked, chunked,
        chunked, chunked, vmem((2, K, C, R, Y), F32), vmem((2, K, C, R, Y), F32),
        vmem((L, C, X + 16, Y), F32),
        vmem((L * C, Y), F32), vmem((L * C, Y), F32), vmem((X, LANES), F32), vmem((X, LANES), F32),
        dma((4,)), dma((S,)), dma((S,)), dma, dma, dma((K,)), dma((K,)),
        dma((K,)), dma((K,)), dma((K,)), dma((K,)), dma((K,)), dma((K,)), dma((K,)), dma((K,)),
        dma, dma, dma, dma,
    ]
    any_space = pl.BlockSpec(memory_space=pl.ANY)
    in_vmem = pl.BlockSpec(memory_space=pltpu.VMEM)
    return pl.pallas_call(
        functools.partial(kernel, (S, L, C, X, Y, K)),
        out_shape=jax.ShapeDtypeStruct(source.shape, F32),
        in_specs=[any_space] * 4 + [in_vmem] * 4,
        out_specs=in_vmem,
        scratch_shapes=scratch,
        compiler_params=pltpu.CompilerParams(
            collective_id=0, has_side_effects=True, vmem_limit_bytes=48 * 1024 * 1024
        ),
    )(
        source, phase, attenuation, pml_level,
        recv_values[0, 0], recv_slab[0, 0], recv_lateral[0], recv_layer[0],
    )


def solution(mesh):
    in_specs = (
        P("slab", None, "px", "py"),
        P("slab", "px", "py"),
        P("slab", "px", "py"),
        P("px", "py"),
        P("px", "py", None, "slab"),
        P("px", "py", "slab", None),
        P("px", "py", "slab"),
        P("px", "py", "slab"),
    )
    out_specs = P("slab", None, "px", "py")
    return jax.shard_map(shards, mesh=mesh, in_specs=in_specs, out_specs=out_specs, check_vma=False)
```

time: 218 us -> 47.7 us (0.22); the launches traced: 215 us -> 47.4 us
  starting transfers between devices: 94 us -> 0 us
  waiting for transfers between devices: 52.8 us -> 0 us
  other arithmetic: 44.6 us -> 0 us
  Pallas kernels: 0 us -> 41.1 us
  local copies, waits for them, and re-layouts: 22.7 us -> 6.31 us
    ppermute x32 -> x0, starting transfers between devices: 83.4 us -> none  [the longest x28 73.2 us: from_behind(): return lax.ppermute(array, axis, pairs)]
    ppermute x32 -> x0, waiting for transfers between devices: 44.9 us -> none  [the longest x28 43.2 us: from_behind(): return lax.ppermute(array, axis, pairs)]
    pallas_call x0 -> x1, Pallas kernels: none -> 41.1 us  [shards(): pl.pallas_call(functools.partial(kernel, (S, L, C, X, Y, K)), out_shape=j...]
    add x24 -> x0, other arithmetic: 18.2 us -> none  [the longest x7 10.9 us: relay_turn(): total_up[0] * below_imag + total_up[1] * below_real + total_up[3]]
    scatter-add x1 -> x0, other arithmetic: 11.9 us -> none  [shards(): forcing = source.reshape(-1).at[flat_index].add(inject_values.reshape(-1))]
    all_to_all x2 -> x0, starting transfers between devices: 10.7 us -> none  [the longest x1 7.28 us: shards(): lax.all_to_all(send_places.reshape(1, slab_count, capacity), 'slab', spli...]
    slice x9 -> x0, local copies, waits for them, and re-layouts: 9.21 us -> none  [the longest x2 3.23 us: padded_2(): lax.slice_in_dim(block, 0, width, axis=dim)]
    all_to_all x2 -> x0, waiting for transfers between devices: 7.89 us -> none  [the longest x1 5.29 us: shards(): lax.all_to_all(send_values.reshape(components, slab_count, capacity), 'sl...]
  transfers between devices with their start and end apart: 34 -> 0, of which waited for: 19 -> 0; matrix products, arithmetic and copies ran while one was open for 8% -> 0% of each run, Pallas kernels for 0% -> 0%
where the time goes in v1:
time: 47.7 us; the launch traced here: 47.4 us
  Pallas kernels  41.1 us (86%)
  local copies, waits for them, and re-layouts  6.31 us (13%)
    pallas_call x1, Pallas kernels, shards(): pl.pallas_call(functools.partial(kernel, (S, L, C, X, Y, K)), out_shape=j...  41.1 us
    unnamed x15, local copies, waits for them, and re-layouts  5.44 us

profile of v1, /device:TPU:0, one launch (start us, length us, event | category | flops | bytes accessed | tf_op | source)
XLA Modules:
  0.0 47.4 jit_solution(3119346449621523953)
XLA Ops:
  0.0 0.0 copy-start.1
  0.0 0.0 copy-start.4
  0.0 0.9 %copy.9.rslab = s32[512,1]{1,0:T(8,128)S(1)} copy(s32[512,1]{0,1:T(1,128)} %bitcast.7) | data formatting | bytes 4096 | tf_op jit(solution)/shard_map/squeeze | solution.py:413
  0.9 0.1 copy-done.1
  1.0 0.0 copy-done.4
  1.0 0.0 copy-start
  1.0 1.2 %copy-done = f32[4,4,128,128]{3,2,1,0:T(8,128)S(1)} copy-done((f32[4,4,128,128]{3,2,1,0:T(8,128)S(1)}, f32[4,4,128,128]{3,2,1,0:T(8,128)}, u32[]{:S(2)}) %copy-start) | copy-done | bytes 1048600
  2.2 0.0 copy-start.2
  2.2 0.9 %copy-done.2 = f32[4,128,128]{2,1,0:T(8,128)S(1)} copy-done((f32[4,128,128]{2,1,0:T(8,128)S(1)}, f32[4,128,128]{2,1,0:T(8,128)}, u32[]{:S(2)}) %copy-start.2) | copy-done | bytes 262168
  3.1 0.0 copy-start.3
  3.1 0.8 %copy-done.3 = s32[128,128]{1,0:T(8,128)S(1)} copy-done((s32[128,128]{1,0:T(8,128)S(1)}, s32[128,128]{1,0:T(8,128)}, u32[]{:S(2)}) %copy-start.3) | copy-done | bytes 65560
  4.0 0.0 copy-start.5
  4.0 0.7 %copy-done.5 = s32[1,1,512]{2,1,0:T(1,128)S(1)} copy-done((s32[1,1,512]{2,1,0:T(1,128)S(1)}, s32[1,1,512]{2,1,0:T(1,128)}, u32[]{:S(2)}) %copy-start.5) | copy-done | bytes 2072
  4.7 0.0 copy-start.6
  4.7 0.7 %copy-done.6 = s32[1,1,512]{2,1,0:T(1,128)S(1)} copy-done((s32[1,1,512]{2,1,0:T(1,128)S(1)}, s32[1,1,512]{2,1,0:T(1,128)}, u32[]{:S(2)}) %copy-start.6) | copy-done | bytes 2072
  5.3 41.1 %shard_map.82 = f32[4,4,128,128]{3,2,1,0:T(8,128)S(1)} custom-call(f32[4,4,128,128]{3,2,1,0:T(8,128)S(1)} %copy-done, f32[4,128,128]{2,1,0:T(8,128)S(1)} %copy-done.1, f32[4,128,128]{2,1,0:T(8,128)S(1)} %copy-done.2, s32[128,128]{1,0:T(8,128)S(1)} %copy-done.3, f32[4,512]{1,0:T(4,128)S(1)} %bitcast.4, s32[512,1]{1,0:T(8,128)S(1)} %copy.9.rslab, ...), custom_call_target="tpu_custom_call" | custom-call | tf_op jit(solution)/shard_map/pallas_call | solution.py:402
  46.4 1.0 %copy.11 = f32[4,4,128,128]{3,2,1,0:T(8,128)} copy(f32[4,4,128,128]{3,2,1,0:T(8,128)S(1)} %shard_map.82) | data formatting | bytes 2097152
Async XLA Ops:
  0.0 1.0 %copy-start.1 = (f32[4,128,128]{2,1,0:T(8,128)S(1)}, f32[4,128,128]{2,1,0:T(8,128)}, u32[]{:S(2)}) copy-start(f32[4,128,128]{2,1,0:T(8,128)} %phase_hbm.1) | copy-start | bytes 786436
  0.0 1.0 %copy-start.4 = (f32[1,1,4,512]{3,2,1,0:T(4,128)S(1)}, f32[1,1,4,512]{3,2,1,0:T(4,128)}, u32[]{:S(2)}) copy-start(f32[1,1,4,512]{3,2,1,0:T(4,128)} %param.12) | copy-start | bytes 24580
  1.0 1.2 %copy-start = (f32[4,4,128,128]{3,2,1,0:T(8,128)S(1)}, f32[4,4,128,128]{3,2,1,0:T(8,128)}, u32[]{:S(2)}) copy-start(f32[4,4,128,128]{3,2,1,0:T(8,128)} %src_hbm.1) | copy-start | bytes 3145732
  2.2 0.9 %copy-start.2 = (f32[4,128,128]{2,1,0:T(8,128)S(1)}, f32[4,128,128]{2,1,0:T(8,128)}, u32[]{:S(2)}) copy-start(f32[4,128,128]{2,1,0:T(8,128)} %att_hbm.1) | copy-start | bytes 786436
  3.1 0.8 %copy-start.3 = (s32[128,128]{1,0:T(8,128)S(1)}, s32[128,128]{1,0:T(8,128)}, u32[]{:S(2)}) copy-start(s32[128,128]{1,0:T(8,128)} %pml_hbm.1) | copy-start | bytes 196612
  4.0 0.7 %copy-start.5 = (s32[1,1,512]{2,1,0:T(1,128)S(1)}, s32[1,1,512]{2,1,0:T(1,128)}, u32[]{:S(2)}) copy-start(s32[1,1,512]{2,1,0:T(1,128)} %param.14) | copy-start | bytes 6148
  4.7 0.7 %copy-start.6 = (s32[1,1,512]{2,1,0:T(1,128)S(1)}, s32[1,1,512]{2,1,0:T(1,128)}, u32[]{:S(2)}) copy-start(s32[1,1,512]{2,1,0:T(1,128)} %param.15) | copy-start | bytes 6148

commit v2 on v1

--- a/solution.py
+++ b/solution.py
@@ -10,6 +10,7 @@
 CHUNKS = 4
 LANES = 128
 CAP = 64
+VMEM_BYTES = 60 * 1024 * 1024
 BF16 = jnp.bfloat16
 F32 = jnp.float32
 
@@ -26,12 +27,24 @@
     return rate[0] * state[0] - rate[1] * state[1], rate[0] * state[1] + rate[1] * state[0]
 
 
+def circle(angle):
+    t = (angle - 1.5707963705062866) + 4.371139000186241e-08
+    z = t * t
+    odd = -1.0 / 39916800.0
+    for factor in (1.0 / 362880.0, -1.0 / 5040.0, 1.0 / 120.0, -1.0 / 6.0):
+        odd = odd * z + factor
+    even = 1.0 / 479001600.0
+    for factor in (-1.0 / 3628800.0, 1.0 / 40320.0, -1.0 / 720.0, 1.0 / 24.0, -0.5):
+        even = even * z + factor
+    return -(t + t * z * odd), 1.0 + z * even
+
+
 def kernel(
     sizes,
-    src_hbm, phase_hbm, att_hbm, pml_hbm, vals, rslab, rlat, rlay,
+    src_hbm, phase_hbm, att_hbm, pml_hbm, vals_hbm, slab_hbm, lat_hbm, lay_hbm,
     out,
-    force, phase, att, pml, rate_re, rate_im,
-    data, spread, arrived, left, right,
+    vals, rslab, rlat, rlay, force, phase, att, pml, rate_re, rate_im,
+    data, spread, arrived, right,
     prod_send, prod_pair, fwd_send, pair,
     down_send, down_recv, up_send, up_recv,
     down_back, up_back, enter_down, enter_up,
@@ -68,37 +81,55 @@
     loads = [
         pltpu.make_async_copy(a, b, in_sem.at[i])
         for i, (a, b) in enumerate(
-            ((phase_hbm, phase), (att_hbm, att), (pml_hbm, pml), (src_hbm, force))
+            (
+                (slab_hbm, rslab), (vals_hbm, vals), (lat_hbm, rlat), (lay_hbm, rlay),
+                (phase_hbm, phase), (att_hbm, att), (pml_hbm, pml), (src_hbm, force),
+            )
         )
     ]
     for load in loads:
         load.start()
 
+    for load in loads[:4]:
+        load.wait()
     rows = vals.shape[1]
-    lane = lax.broadcasted_iota(jnp.int32, (rows, LANES), 1)
+    blocks = rows // LANES
     slab_of = rslab[...]
-    hot = jnp.where(lane == slab_of, 1.0, 0.0)
+    hot = jnp.where(lax.broadcasted_iota(jnp.int32, (S, rows), 0) == slab_of, 1.0, 0.0)
+    cuts = [hot[:, i * LANES : (i + 1) * LANES] for i in range(blocks)]
     earlier = jnp.where(
-        lax.broadcasted_iota(jnp.int32, (rows, rows), 1)
-        < lax.broadcasted_iota(jnp.int32, (rows, rows), 0),
+        lax.broadcasted_iota(jnp.int32, (LANES, LANES), 0)
+        < lax.broadcasted_iota(jnp.int32, (LANES, LANES), 1),
         1.0, 0.0,
     ).astype(BF16)
-    before = jnp.dot(earlier, hot.astype(BF16), preferred_element_type=F32)
-    rank = jnp.sum(before * hot, axis=1, keepdims=True).astype(jnp.int32)
-    slot = slab_of * LANES + rank
-    place = jnp.where(
-        lax.broadcasted_iota(jnp.int32, (rows, S * LANES), 1) == slot, 1.0, 0.0
-    ).astype(BF16)
+    within = jnp.dot(
+        jnp.concatenate(cuts, axis=0).astype(BF16), earlier, preferred_element_type=F32
+    )
+    passed = jnp.zeros((S, 1), F32)
+    ranks = []
+    for i in range(blocks):
+        ranks.append(
+            jnp.sum((within[i * S : (i + 1) * S] + passed) * cuts[i], axis=0, keepdims=True)
+        )
+        passed = passed + jnp.sum(cuts[i], axis=1, keepdims=True)
+    slot = slab_of * LANES + jnp.concatenate(ranks, axis=1).astype(jnp.int32)
     lateral = rlat[...]
     data[...] = jnp.zeros_like(data)
     data[0:C, :] = vals[...]
     data[C : C + 1, :] = (rlay[...] * X + lax.div(lateral, Y)).astype(F32)
     data[C + 1 : C + 2, :] = lax.rem(lateral, Y).astype(F32)
-    routed = sum(
-        jnp.dot(part, place, preferred_element_type=F32) for part in thirds(data[...])
-    )
-    for s in range(S):
-        spread[s] = routed[:, s * LANES : (s + 1) * LANES]
+    pieces = jnp.concatenate([part.astype(F32) for part in thirds(data[...])], axis=0).astype(BF16)
+    slot_at = lax.broadcasted_iota(jnp.int32, (LANES, rows), 0)
+
+    def route(s, carry):
+        place = jnp.where(slot_at + s * LANES == slot, 1.0, 0.0).astype(BF16)
+        routed = lax.dot_general(
+            pieces, place, (((1,), (1,)), ((), ())), preferred_element_type=F32
+        )
+        spread[s] = routed[0:8] + routed[8:16] + routed[16:24]
+        return carry
+
+    lax.fori_loop(0, S, route, 0)
 
     pl.semaphore_wait(barrier, S + 1)
     arrived[me] = spread[me]
@@ -110,13 +141,18 @@
         copy.start()
         spreads.append(copy)
 
-    for load in loads[:3]:
+    for load in loads[4:7]:
         load.wait()
-    for l in range(L):
+
+    def rate(l, carry):
         damping = att[l] + (0.5 / (L * S)) * pml[...].astype(F32)
         amplitude = jnp.exp(-damping)
-        rate_re[l] = amplitude * jnp.cos(phase[l])
-        rate_im[l] = amplitude * jnp.sin(phase[l])
+        cosine, sine = circle(phase[l])
+        rate_re[l] = amplitude * cosine
+        rate_im[l] = amplitude * sine
+        return carry
+
+    lax.fori_loop(0, L, rate, 0)
 
     def product(half):
         at = pl.ds(pl.multiple_of(half * H, H), H)
@@ -134,7 +170,6 @@
     prod_pair[y, 0] = total[0]
     prod_pair[y, 1] = total[1]
 
-    loads[3].wait()
     for peer in peers:
         remote(
             spread.at[peer], arrived.at[peer], spread_s.at[peer], spread_r.at[peer], {"slab": peer}
@@ -145,25 +180,27 @@
     )
     row_at = got[C : C + 1, :].astype(jnp.int32)
     col_at = got[C + 1 : C + 2, :].astype(jnp.int32)
-    on_row = jnp.where(
-        lax.broadcasted_iota(jnp.int32, (L * X, slots), 0) == row_at, 1.0, 0.0
-    ).astype(BF16)
+    x_at = lax.broadcasted_iota(jnp.int32, (X, slots), 0)
     on_col = lax.broadcasted_iota(jnp.int32, (Y, slots), 0) == col_at
-    parts = thirds(got)
+    parts = [part.astype(F32) for part in thirds(got)]
     for i in range(3):
-        left[:, i * slots : (i + 1) * slots] = on_row
-        part = parts[i].astype(F32)
         for c in range(C):
             right[c * Y : (c + 1) * Y, i * slots : (i + 1) * slots] = jnp.where(
-                on_col, part[c : c + 1, :], 0.0
+                on_col, parts[i][c : c + 1, :], 0.0
             ).astype(BF16)
-    for l in range(L):
+    loads[7].wait()
+
+    def inject(l, carry):
+        on_row = jnp.where(x_at + l * X == row_at, 1.0, 0.0).astype(BF16)
         added = lax.dot_general(
-            left[l * X : (l + 1) * X, :], right[...], (((1,), (1,)), ((), ())),
+            jnp.concatenate([on_row] * 3, axis=1), right[...], (((1,), (1,)), ((), ())),
             preferred_element_type=F32,
         )
         for c in range(C):
             force[l, c] += added[:, c * Y : (c + 1) * Y]
+        return carry
+
+    lax.fori_loop(0, L, inject, 0)
 
     def local(half, k, dst):
         at = pl.ds(pl.multiple_of(half * H + k * R, R), R)
@@ -183,14 +220,51 @@
             dst[C + 2 * s] = v[0]
             dst[C + 2 * s + 1] = v[1]
 
-    sends = []
-    for k in range(K):
+    def fwd_copy(k):
+        return remote(fwd_send.at[k], pair.at[y, k], fwd_s.at[k], fwd_r.at[k], partner)
+
+    def give(k, carry):
         local(1 - y, k, fwd_send.at[k])
-        copy = remote(fwd_send.at[k], pair.at[y, k], fwd_s.at[k], fwd_r.at[k], partner)
-        copy.start()
-        sends.append(copy)
-    for k in range(K):
+        fwd_copy(k).start()
+        return carry
+
+    def keep(k, carry):
         local(y, k, pair.at[y, k])
+        return carry
+
+    lax.fori_loop(0, K, give, 0)
+    lax.fori_loop(0, K, keep, 0)
+
+    pad = comb.shape[1] // 2 - X // 2
+    column = jnp.where(py == 0, Y - 1, 0)
+    chunk_lane = lax.broadcasted_iota(jnp.int32, (R, LANES), 1)
+
+    def full(half, k):
+        row = half * H + k * R
+        at = pl.ds(pl.multiple_of(row, R), R)
+        to = pl.ds(pl.multiple_of(row + pad, 8), R)
+        rates = [(rate_re[l, at], rate_im[l, at]) for l in range(L)]
+        held = jnp.zeros((R, LANES), F32)
+        for s in range(shots):
+            i, j = 2 * s, 2 * s + 1
+            f = [(force[l, i, at], force[l, j, at]) for l in range(L)]
+            w = (enter_down[half, k, i], enter_down[half, k, j])
+            downs = []
+            for l in range(L):
+                re, im = times(rates[l], w)
+                w = (re + f[l][0], im + f[l][1])
+                downs.append(w)
+            v = (enter_up[half, k, i], enter_up[half, k, j])
+            for l in range(L - 1, -1, -1):
+                turn = times(rates[l], v)
+                for a in (0, 1):
+                    plane = l * C + i + a
+                    value = downs[l][a] + turn[a]
+                    comb[plane, to] = value
+                    shift = lax.rem(plane + LANES - column, LANES)
+                    held = jnp.where(chunk_lane == plane, pltpu.roll(value, shift, 1), held)
+                v = (turn[0] + f[l][0], turn[1] + f[l][1])
+        col_send[at] = held
 
     @pl.when(g == 0)
     def _():
@@ -231,8 +305,11 @@
                 theirs[k, 2 * s + a] = jnp.where(own_direct, q[a], e[a])
 
     send_prod.wait_recv()
-    for t in range(K + G - 1):
-        if t < K:
+    ready = jnp.maximum(g, G - 1 - g)
+
+    def chain(t, carry):
+        @pl.when(t < K)
+        def _():
             remote(
                 fwd_send.at[t], pair.at[1 - y, t], fwd_s.at[t], fwd_r.at[t], partner
             ).wait_recv()
@@ -271,32 +348,17 @@
 
             up_back_copy(ku).start()
 
-    pad = comb.shape[2] // 2 - X // 2
-
-    def full(half, k):
-        row = half * H + k * R
-        at = pl.ds(pl.multiple_of(row, R), R)
-        to = pl.ds(pl.multiple_of(row + pad, 8), R)
-        rates = [(rate_re[l, at], rate_im[l, at]) for l in range(L)]
-        for s in range(shots):
-            i, j = 2 * s, 2 * s + 1
-            f = [(force[l, i, at], force[l, j, at]) for l in range(L)]
-            w = (enter_down[half, k, i], enter_down[half, k, j])
-            downs = []
-            for l in range(L):
-                re, im = times(rates[l], w)
-                w = (re + f[l][0], im + f[l][1])
-                downs.append(w)
-            v = (enter_up[half, k, i], enter_up[half, k, j])
-            for l in range(L - 1, -1, -1):
-                re, im = times(rates[l], v)
-                comb[l, i, to] = downs[l][0] + re
-                comb[l, j, to] = downs[l][1] + im
-                v = (re + f[l][0], im + f[l][1])
-
-    for k in range(K):
-        full(y, k)
-    for k in range(K):
+        ke = t - ready
+
+        @pl.when((ke >= 0) & (ke < K))
+        def _():
+            full(y, ke)
+
+        return carry
+
+    lax.fori_loop(0, K + G - 1, chain, 0)
+
+    def finish(k, carry):
         remote(
             down_back.at[k], enter_down.at[1 - y, k], dback_s.at[k], dback_r.at[k], partner
         ).wait_recv()
@@ -304,42 +366,46 @@
             up_back.at[k], enter_up.at[1 - y, k], uback_s.at[k], uback_r.at[k], partner
         ).wait_recv()
         full(1 - y, k)
-
-    edge_lane = lax.broadcasted_iota(jnp.int32, (X, LANES), 1)
+        return carry
+
+    lax.fori_loop(0, K, finish, 0)
+
+    cols_out = remote(col_send, col_recv, col_s, col_r, other_y)
+    cols_out.start()
+    planes = L * C
 
     def send_rows(row):
-        for l in range(L):
-            for c in range(C):
-                row_send[l * C + c : l * C + c + 1, :] = comb[l, c, pad + row : pad + row + 1, :]
-
-    def send_cols(col):
-        held = jnp.zeros((X, LANES), F32)
-        for l in range(L):
-            for c in range(C):
-                column = comb[l, c, pad : pad + X, col : col + 1]
-                held = jnp.where(edge_lane == l * C + c, column, held)
-        col_send[...] = held
+        for i in range(planes):
+            row_send[i : i + 1, :] = comb[i, pad + row : pad + row + 1, :]
 
     pl.when(px == 0)(lambda: send_rows(X - 1))
     pl.when(px == 1)(lambda: send_rows(0))
     rows_out = remote(row_send, row_recv, row_s, row_r, other_x)
     rows_out.start()
-    pl.when(py == 0)(lambda: send_cols(Y - 1))
-    pl.when(py == 1)(lambda: send_cols(0))
-    cols_out = remote(col_send, col_recv, col_s, col_r, other_y)
-    cols_out.start()
 
     full_lane = lax.broadcasted_iota(jnp.int32, (X, Y), 1)
-    for l in range(L):
-        for c in range(C):
-            comb[l, c, pad - 1 : pad, :] = jnp.zeros((1, Y), F32)
-            comb[l, c, pad + X : pad + X + 1, :] = jnp.zeros((1, Y), F32)
-            here = comb[l, c, pad : pad + X, :]
-            around = comb[l, c, pad - 1 : pad - 1 + X, :] + comb[l, c, pad + 1 : pad + 1 + X, :]
-            around += jnp.where(full_lane == 0, 0.0, pltpu.roll(here, 1, 1))
-            around += jnp.where(full_lane == Y - 1, 0.0, pltpu.roll(here, Y - 1, 1))
-            out[l, c] = here - 0.2 * (4.0 * here - around)
-
+
+    def stencil(i, carry):
+        comb[i, pad - 1 : pad, :] = jnp.zeros((1, Y), F32)
+        comb[i, pad + X : pad + X + 1, :] = jnp.zeros((1, Y), F32)
+        here = comb[i, pad : pad + X, :]
+        around = comb[i, pad - 1 : pad - 1 + X, :] + comb[i, pad + 1 : pad + 1 + X, :]
+        around += jnp.where(full_lane == 0, 0.0, pltpu.roll(here, 1, 1))
+        around += jnp.where(full_lane == Y - 1, 0.0, pltpu.roll(here, Y - 1, 1))
+        out[lax.div(i, C), lax.rem(i, C)] = here - 0.2 * (4.0 * here - around)
+        return carry
+
+    lax.fori_loop(0, planes, stencil, 0)
+    cols_out.wait_recv()
+    at_edge = full_lane == column
+
+    def add_columns(i, carry):
+        shift = lax.rem(column + LANES - i, LANES)
+        moved = pltpu.roll(col_recv[...], shift, 1)
+        out[lax.div(i, C), lax.rem(i, C)] += jnp.where(at_edge, 0.2 * moved, 0.0)
+        return carry
+
+    lax.fori_loop(0, planes, add_columns, 0)
     rows_out.wait_recv()
 
     def add_rows(row):
@@ -349,16 +415,11 @@
 
     pl.when(px == 0)(lambda: add_rows(X - 1))
     pl.when(px == 1)(lambda: add_rows(0))
-    cols_out.wait_recv()
-    at_edge = full_lane == jnp.where(py == 0, Y - 1, 0)
-    for l in range(L):
-        for c in range(C):
-            i = l * C + c
-            out[l, c] += jnp.where(at_edge, 0.2 * col_recv[:, i : i + 1], 0.0)
-
-    for copy in spreads + sends + [send_prod, rows_out, cols_out]:
+
+    for copy in spreads + [send_prod, rows_out, cols_out]:
         copy.wait_send()
     for k in range(K):
+        fwd_copy(k).wait_send()
         down_back_copy(k).wait_send()
         up_back_copy(k).wait_send()
 
@@ -383,17 +444,18 @@
     vmem, dma = pltpu.VMEM, pltpu.SemaphoreType.DMA
     chunked = vmem((K, C, R, Y), F32)
     scratch = [
+        vmem((C, rows), F32), vmem((1, rows), jnp.int32), vmem((1, rows), jnp.int32), vmem((1, rows), jnp.int32),
         vmem((L, C, X, Y), F32), vmem((L, X, Y), F32), vmem((L, X, Y), F32), vmem((X, Y), jnp.int32),
         vmem((L, X, Y), F32), vmem((L, X, Y), F32),
         vmem((8, rows), F32), vmem((S, 8, LANES), F32), vmem((S, 8, LANES), F32),
-        vmem((L * X, 3 * S * CAP), BF16), vmem((C * Y, 3 * S * CAP), BF16),
+        vmem((C * Y, 3 * S * CAP), BF16),
         vmem((2, H, Y), F32), vmem((2, 2, H, Y), F32),
         vmem((K, 2 * C, R, Y), F32), vmem((2, K, 2 * C, R, Y), F32),
         chunked, chunked, chunked, chunked,
         chunked, chunked, vmem((2, K, C, R, Y), F32), vmem((2, K, C, R, Y), F32),
-        vmem((L, C, X + 16, Y), F32),
+        vmem((L * C, X + 16, Y), F32),
         vmem((L * C, Y), F32), vmem((L * C, Y), F32), vmem((X, LANES), F32), vmem((X, LANES), F32),
-        dma((4,)), dma((S,)), dma((S,)), dma, dma, dma((K,)), dma((K,)),
+        dma((8,)), dma((S,)), dma((S,)), dma, dma, dma((K,)), dma((K,)),
         dma((K,)), dma((K,)), dma((K,)), dma((K,)), dma((K,)), dma((K,)), dma((K,)), dma((K,)),
         dma, dma, dma, dma,
     ]
@@ -402,15 +464,15 @@
     return pl.pallas_call(
         functools.partial(kernel, (S, L, C, X, Y, K)),
         out_shape=jax.ShapeDtypeStruct(source.shape, F32),
-        in_specs=[any_space] * 4 + [in_vmem] * 4,
+        in_specs=[any_space] * 8,
         out_specs=in_vmem,
         scratch_shapes=scratch,
         compiler_params=pltpu.CompilerParams(
-            collective_id=0, has_side_effects=True, vmem_limit_bytes=48 * 1024 * 1024
+            collective_id=0, has_side_effects=True, vmem_limit_bytes=VMEM_BYTES
         ),
     )(
         source, phase, attenuation, pml_level,
-        recv_values[0, 0], recv_slab[0, 0], recv_lateral[0], recv_layer[0],
+        recv_values[0, 0], recv_slab.reshape(1, rows), recv_lateral[0], recv_layer[0],
     )
 
 

time: 47.7 us -> 45.1 us (0.945)
  local copies, waits for them, and re-layouts: 6.31 us -> 2.3 us
  Pallas kernels: 41.1 us -> 42.6 us
    unnamed x15 -> x1, local copies, waits for them, and re-layouts: 5.44 us -> 2.3 us
    pallas_call x1, Pallas kernels: 41.1 us -> 42.6 us  [shards(): pl.pallas_call(functools.partial(kernel, (S, L, C, X, Y, K)), out_shape=j...]
    squeeze x1 -> x0, local copies, waits for them, and re-layouts: 0.86 us -> none  [shards(): recv_slab[0, 0]]
where the time goes in v2:
time: 45.1 us; the launch traced here: 44.9 us
  Pallas kernels  42.6 us (94%)
  local copies, waits for them, and re-layouts  2.3 us (5%)
    pallas_call x1, Pallas kernels, shards(): pl.pallas_call(functools.partial(kernel, (S, L, C, X, Y, K)), out_shape=j...  42.6 us
    unnamed x1, local copies, waits for them, and re-layouts  2.3 us

profile of v2, /device:TPU:0, one launch (start us, length us, event | category | flops | bytes accessed | tf_op | source)
XLA Modules:
  0.0 44.9 jit_solution(924184637391062180)
XLA Ops:
  0.0 42.6 %shard_map.82 = f32[4,4,128,128]{3,2,1,0:T(8,128)} custom-call(f32[4,4,128,128]{3,2,1,0:T(8,128)} %src_hbm.1, f32[4,128,128]{2,1,0:T(8,128)} %phase_hbm.1, f32[4,128,128]{2,1,0:T(8,128)} %att_hbm.1, s32[128,128]{1,0:T(8,128)} %pml_hbm.1, f32[4,512]{1,0:T(4,128)} %bitcast.4, s32[1,512]{1,0:T(1,128)} %bitcast.5, s32[1,512]{1,0:T(1,128)} %bitcast.6, ...), custom_call_target="tpu_custom_call" | custom-call | tf_op jit(solution)/shard_map/pallas_call | solution.py:464
  42.7 2.3 %copy.10 = f32[4,4,128,128]{3,2,1,0:T(8,128)} copy(f32[4,4,128,128]{3,2,1,0:T(8,128)} %shard_map.82) | data formatting | bytes 2097152

commit v3 on v2

--- a/solution.py
+++ b/solution.py
@@ -7,10 +7,11 @@
 from jax.experimental.pallas import tpu as pltpu
 from jax.sharding import PartitionSpec as P
 
-CHUNKS = 4
+GROUP = 4
+CHUNKS = 2
 LANES = 128
 CAP = 64
-VMEM_BYTES = 60 * 1024 * 1024
+VMEM_BYTES = 48 * 1024 * 1024
 BF16 = jnp.bfloat16
 F32 = jnp.float32
 
@@ -45,7 +46,7 @@
     out,
     vals, rslab, rlat, rlay, force, phase, att, pml, rate_re, rate_im,
     data, spread, arrived, right,
-    prod_send, prod_pair, fwd_send, pair,
+    prod_send, prod_all, fwd_send, gathered,
     down_send, down_recv, up_send, up_recv,
     down_back, up_back, enter_down, enter_up,
     comb, row_send, row_recv, col_send, col_recv,
@@ -53,19 +54,25 @@
     down_s, down_r, up_s, up_r, dback_s, dback_r, uback_s, uback_r,
     row_s, row_r, col_s, col_r,
 ):
-    S, L, C, X, Y, K = sizes
-    G = S // 2
-    H = X // 2
+    S, L, C, X, Y, K, M = sizes
+    G = S // M
+    H = X // M
     R = H // K
     shots = C // 2
     me = lax.axis_index("slab")
     px = lax.axis_index("px")
     py = lax.axis_index("py")
-    g = lax.div(me, 2)
-    y = lax.rem(me, 2)
-    partner = {"slab": g * 2 + (1 - y)}
+    g = lax.div(me, M)
+    m = lax.rem(me, M)
+    fellows = M - 1
     other_x = {"px": 1 - px}
     other_y = {"py": 1 - py}
+
+    def fellow(step):
+        return lax.rem(m + step, M)
+
+    def place_of(member):
+        return {"slab": g * M + member}
 
     def remote(src, dst, send, recv, where):
         return pltpu.make_async_remote_copy(
@@ -161,14 +168,23 @@
             total = times((rate_re[l, at], rate_im[l, at]), total)
         return total
 
-    total = product(1 - y)
-    prod_send[0] = total[0]
-    prod_send[1] = total[1]
-    send_prod = remote(prod_send, prod_pair.at[y], prod_s, prod_r, partner)
-    send_prod.start()
-    total = product(y)
-    prod_pair[y, 0] = total[0]
-    prod_pair[y, 1] = total[1]
+    def prod_copy(j, source):
+        return remote(
+            prod_send.at[j], prod_all.at[source], prod_s.at[j], prod_r.at[source], place_of(j)
+        )
+
+    def give_product(step, carry):
+        j = fellow(step)
+        total = product(j)
+        prod_send[j, 0] = total[0]
+        prod_send[j, 1] = total[1]
+        prod_copy(j, m).start()
+        return carry
+
+    lax.fori_loop(1, M, give_product, 0)
+    total = product(m)
+    prod_all[m, 0] = total[0]
+    prod_all[m, 1] = total[1]
 
     for peer in peers:
         remote(
@@ -220,19 +236,23 @@
             dst[C + 2 * s] = v[0]
             dst[C + 2 * s + 1] = v[1]
 
-    def fwd_copy(k):
-        return remote(fwd_send.at[k], pair.at[y, k], fwd_s.at[k], fwd_r.at[k], partner)
-
-    def give(k, carry):
-        local(1 - y, k, fwd_send.at[k])
-        fwd_copy(k).start()
+    def fwd_copy(j, k, source):
+        return remote(
+            fwd_send.at[j, k], gathered.at[source, k], fwd_s.at[j, k], fwd_r.at[source, k],
+            place_of(j),
+        )
+
+    def give(i, carry):
+        k, j = lax.div(i, fellows), fellow(1 + lax.rem(i, fellows))
+        local(j, k, fwd_send.at[j, k])
+        fwd_copy(j, k, m).start()
         return carry
 
     def keep(k, carry):
-        local(y, k, pair.at[y, k])
-        return carry
-
-    lax.fori_loop(0, K, give, 0)
+        local(m, k, gathered.at[m, k])
+        return carry
+
+    lax.fori_loop(0, K * fellows, give, 0)
     lax.fori_loop(0, K, keep, 0)
 
     pad = comb.shape[1] // 2 - X // 2
@@ -274,101 +294,106 @@
     def _():
         up_recv[...] = jnp.zeros_like(up_recv)
 
-    def down_copy(k):
-        return remote(down_send.at[k], down_recv.at[k], down_s.at[k], down_r.at[k], {"slab": me + 2})
-
-    def up_copy(k):
-        return remote(up_send.at[k], up_recv.at[k], up_s.at[k], up_r.at[k], {"slab": me - 2})
-
-    def down_back_copy(k):
-        return remote(down_back.at[k], enter_down.at[y, k], dback_s.at[k], dback_r.at[k], partner)
-
-    def up_back_copy(k):
-        return remote(up_back.at[k], enter_up.at[y, k], uback_s.at[k], uback_r.at[k], partner)
-
-    def factors(k, member):
+    def down_copy(k, to):
+        return remote(down_send.at[k], down_recv.at[k], down_s.at[k], down_r.at[k], {"slab": to})
+
+    def up_copy(k, to):
+        return remote(up_send.at[k], up_recv.at[k], up_s.at[k], up_r.at[k], {"slab": to})
+
+    def down_back_copy(j, k, source):
+        return remote(
+            down_back.at[j, k], enter_down.at[source, k], dback_s.at[j, k], dback_r.at[source, k],
+            place_of(j),
+        )
+
+    def up_back_copy(j, k, source):
+        return remote(
+            up_back.at[j, k], enter_up.at[source, k], uback_s.at[j, k], uback_r.at[source, k],
+            place_of(j),
+        )
+
+    def hop(k, order, base, incoming, outgoing, back, own):
         at = pl.ds(pl.multiple_of(k * R, R), R)
-        return prod_pair[member, 0, at], prod_pair[member, 1, at]
-
-    def hop(k, first, second, base, incoming, outgoing, own, theirs, own_direct):
-        near, far = factors(k, first), factors(k, second)
         for s in range(shots):
             i, j = 2 * s, 2 * s + 1
             e = (incoming[k, i], incoming[k, j])
-            re, im = times(near, e)
-            q = (re + pair[first, k, base + i], im + pair[first, k, base + j])
-            re, im = times(far, q)
-            outgoing[k, i] = re + pair[second, k, base + i]
-            outgoing[k, j] = im + pair[second, k, base + j]
-            for a in (0, 1):
-                own[y, k, 2 * s + a] = jnp.where(own_direct, e[a], q[a])
-                theirs[k, 2 * s + a] = jnp.where(own_direct, q[a], e[a])
-
-    send_prod.wait_recv()
+            for member in order:
+                back[member, k, i] = e[0]
+                back[member, k, j] = e[1]
+                re, im = times((prod_all[member, 0, at], prod_all[member, 1, at]), e)
+                e = (re + gathered[member, k, base + i], im + gathered[member, k, base + j])
+            outgoing[k, i] = e[0]
+            outgoing[k, j] = e[1]
+        own[m, k] = back[m, k]
+
+    def take_products(step, carry):
+        j = fellow(step)
+        prod_copy(j, j).wait_recv()
+        return carry
+
+    lax.fori_loop(1, M, take_products, 0)
     ready = jnp.maximum(g, G - 1 - g)
 
     def chain(t, carry):
         @pl.when(t < K)
         def _():
-            remote(
-                fwd_send.at[t], pair.at[1 - y, t], fwd_s.at[t], fwd_r.at[t], partner
-            ).wait_recv()
+            for step in range(1, M):
+                j = fellow(step)
+                fwd_copy(j, t, j).wait_recv()
+
         kd = t - g
         ku = t - (G - 1 - g)
-
-        @pl.when((kd >= 0) & (kd < K))
+        has_down = (kd >= 0) & (kd < K)
+        has_up = (ku >= 0) & (ku < K)
+
+        @pl.when(has_down)
         def _():
             @pl.when(g > 0)
             def _():
-                remote(
-                    down_send.at[kd], down_recv.at[kd], down_s.at[kd], down_r.at[kd], {"slab": me - 2}
-                ).wait_recv()
-
-            hop(kd, 0, 1, 0, down_recv, down_send, enter_down, down_back, y == 0)
+                down_copy(kd, me - M).wait_recv()
+
+            hop(kd, range(M), 0, down_recv, down_send, down_back, enter_down)
 
             @pl.when(g < G - 1)
             def _():
-                down_copy(kd).start()
-
-            down_back_copy(kd).start()
-
-        @pl.when((ku >= 0) & (ku < K))
+                down_copy(kd, me + M).start()
+
+            for step in range(1, M):
+                down_back_copy(fellow(step), kd, m).start()
+
+        @pl.when(has_up)
         def _():
             @pl.when(g < G - 1)
             def _():
-                remote(
-                    up_send.at[ku], up_recv.at[ku], up_s.at[ku], up_r.at[ku], {"slab": me + 2}
-                ).wait_recv()
-
-            hop(ku, 1, 0, C, up_recv, up_send, enter_up, up_back, y == 1)
+                up_copy(ku, me + M).wait_recv()
+
+            hop(ku, range(M - 1, -1, -1), C, up_recv, up_send, up_back, enter_up)
 
             @pl.when(g > 0)
             def _():
-                up_copy(ku).start()
-
-            up_back_copy(ku).start()
+                up_copy(ku, me - M).start()
+
+            for step in range(1, M):
+                up_back_copy(fellow(step), ku, m).start()
 
         ke = t - ready
 
         @pl.when((ke >= 0) & (ke < K))
         def _():
-            full(y, ke)
+            full(m, ke)
 
         return carry
 
     lax.fori_loop(0, K + G - 1, chain, 0)
 
-    def finish(k, carry):
-        remote(
-            down_back.at[k], enter_down.at[1 - y, k], dback_s.at[k], dback_r.at[k], partner
-        ).wait_recv()
-        remote(
-            up_back.at[k], enter_up.at[1 - y, k], uback_s.at[k], uback_r.at[k], partner
-        ).wait_recv()
-        full(1 - y, k)
-        return carry
-
-    lax.fori_loop(0, K, finish, 0)
+    def finish(i, carry):
+        k, j = lax.div(i, fellows), fellow(1 + lax.rem(i, fellows))
+        down_back_copy(j, k, j).wait_recv()
+        up_back_copy(j, k, j).wait_recv()
+        full(j, k)
+        return carry
+
+    lax.fori_loop(0, K * fellows, finish, 0)
 
     cols_out = remote(col_send, col_recv, col_s, col_r, other_y)
     cols_out.start()
@@ -416,64 +441,75 @@
     pl.when(px == 0)(lambda: add_rows(X - 1))
     pl.when(px == 1)(lambda: add_rows(0))
 
-    for copy in spreads + [send_prod, rows_out, cols_out]:
+    for copy in spreads + [rows_out, cols_out]:
         copy.wait_send()
-    for k in range(K):
-        fwd_copy(k).wait_send()
-        down_back_copy(k).wait_send()
-        up_back_copy(k).wait_send()
+
+    def left(step, carry):
+        j = fellow(step)
+        prod_copy(j, m).wait_send()
+        for k in range(K):
+            fwd_copy(j, k, m).wait_send()
+            down_back_copy(j, k, m).wait_send()
+            up_back_copy(j, k, m).wait_send()
+        return carry
+
+    lax.fori_loop(1, M, left, 0)
 
     @pl.when(g < G - 1)
     def _():
         for k in range(K):
-            down_copy(k).wait_send()
+            down_copy(k, me + M).wait_send()
 
     @pl.when(g > 0)
     def _():
         for k in range(K):
-            up_copy(k).wait_send()
+            up_copy(k, me - M).wait_send()
 
 
 def shards(source, phase, attenuation, pml_level, recv_values, recv_slab, recv_lateral, recv_layer):
     L, C, X, Y = source.shape
     S = lax.axis_size("slab")
     rows = recv_values.shape[3]
-    K = CHUNKS
-    H = X // 2
+    K, M = CHUNKS, GROUP
+    H = X // M
     R = H // K
     vmem, dma = pltpu.VMEM, pltpu.SemaphoreType.DMA
     chunked = vmem((K, C, R, Y), F32)
+    spaced = vmem((M, K, C, R, Y), F32)
     scratch = [
         vmem((C, rows), F32), vmem((1, rows), jnp.int32), vmem((1, rows), jnp.int32), vmem((1, rows), jnp.int32),
         vmem((L, C, X, Y), F32), vmem((L, X, Y), F32), vmem((L, X, Y), F32), vmem((X, Y), jnp.int32),
         vmem((L, X, Y), F32), vmem((L, X, Y), F32),
         vmem((8, rows), F32), vmem((S, 8, LANES), F32), vmem((S, 8, LANES), F32),
         vmem((C * Y, 3 * S * CAP), BF16),
-        vmem((2, H, Y), F32), vmem((2, 2, H, Y), F32),
-        vmem((K, 2 * C, R, Y), F32), vmem((2, K, 2 * C, R, Y), F32),
-        chunked, chunked, chunked, chunked,
-        chunked, chunked, vmem((2, K, C, R, Y), F32), vmem((2, K, C, R, Y), F32),
+        vmem((M, 2, H, Y), F32), vmem((M, 2, H, Y), F32),
+        vmem((M, K, 2 * C, R, Y), F32), vmem((M, K, 2 * C, R, Y), F32),
+        chunked, chunked, chunked, chunked, spaced, spaced, spaced, spaced,
         vmem((L * C, X + 16, Y), F32),
         vmem((L * C, Y), F32), vmem((L * C, Y), F32), vmem((X, LANES), F32), vmem((X, LANES), F32),
-        dma((8,)), dma((S,)), dma((S,)), dma, dma, dma((K,)), dma((K,)),
-        dma((K,)), dma((K,)), dma((K,)), dma((K,)), dma((K,)), dma((K,)), dma((K,)), dma((K,)),
+        dma((8,)), dma((S,)), dma((S,)), dma((M,)), dma((M,)), dma((M, K)), dma((M, K)),
+        dma((K,)), dma((K,)), dma((K,)), dma((K,)),
+        dma((M, K)), dma((M, K)), dma((M, K)), dma((M, K)),
         dma, dma, dma, dma,
     ]
-    any_space = pl.BlockSpec(memory_space=pl.ANY)
+    in_hbm = pl.BlockSpec(memory_space=pltpu.HBM)
     in_vmem = pl.BlockSpec(memory_space=pltpu.VMEM)
     return pl.pallas_call(
-        functools.partial(kernel, (S, L, C, X, Y, K)),
+        functools.partial(kernel, (S, L, C, X, Y, K, M)),
         out_shape=jax.ShapeDtypeStruct(source.shape, F32),
-        in_specs=[any_space] * 8,
+        in_specs=[in_hbm] * 8,
         out_specs=in_vmem,
         scratch_shapes=scratch,
         compiler_params=pltpu.CompilerParams(
             collective_id=0, has_side_effects=True, vmem_limit_bytes=VMEM_BYTES
         ),
-    )(
-        source, phase, attenuation, pml_level,
-        recv_values[0, 0], recv_slab.reshape(1, rows), recv_lateral[0], recv_layer[0],
-    )
+    )(*(
+        pltpu.with_memory_space_constraint(x, pltpu.HBM)
+        for x in (
+            source, phase, attenuation, pml_level,
+            recv_values[0, 0], recv_slab.reshape(1, rows), recv_lateral[0], recv_layer[0],
+        )
+    ))
 
 
 def solution(mesh):

time: 45.1 us -> 34.9 us (0.77)
  Pallas kernels: 42.6 us -> 33.8 us
  local copies, waits for them, and re-layouts: 2.3 us -> 0.97 us
    pallas_call x1, Pallas kernels: 42.6 us -> 33.8 us  [shards(): pl.pallas_call(functools.partial(kernel, (S, L, C, X, Y, K, M)), out_shap...]
    unnamed x1, local copies, waits for them, and re-layouts: 2.3 us -> 0.97 us
where the time goes in v3:
time: 34.9 us; the launch traced here: 34.8 us
  Pallas kernels  33.8 us (97%)
  local copies, waits for them, and re-layouts  0.97 us (3%)
    pallas_call x1, Pallas kernels, shards(): pl.pallas_call(functools.partial(kernel, (S, L, C, X, Y, K, M)), out_shap...  33.8 us
    unnamed x1, local copies, waits for them, and re-layouts  0.97 us

profile of v3, /device:TPU:0, one launch (start us, length us, event | category | flops | bytes accessed | tf_op | source)
XLA Modules:
  0.0 34.8 jit_solution(17931814125063432885)
XLA Ops:
  0.0 33.8 %shard_map.82 = f32[4,4,128,128]{3,2,1,0:T(8,128)S(1)} custom-call(f32[4,4,128,128]{3,2,1,0:T(8,128)} %src_hbm.1, f32[4,128,128]{2,1,0:T(8,128)} %phase_hbm.1, f32[4,128,128]{2,1,0:T(8,128)} %att_hbm.1, s32[128,128]{1,0:T(8,128)} %pml_hbm.1, f32[4,512]{1,0:T(4,128)} %bitcast.4, s32[1,512]{1,0:T(1,128)} %bitcast.5, s32[1,512]{1,0:T(1,128)} %bitcast.6, ...), custom_call_target="tpu_custom_call" | custom-call | tf_op jit(solution)/shard_map/pallas_call | solution.py:497
  33.8 1.0 %copy.10 = f32[4,4,128,128]{3,2,1,0:T(8,128)} copy(f32[4,4,128,128]{3,2,1,0:T(8,128)S(1)} %shard_map.82) | data formatting | bytes 2097152

commit v4 on v3

--- a/solution.py
+++ b/solution.py
@@ -45,7 +45,7 @@
     src_hbm, phase_hbm, att_hbm, pml_hbm, vals_hbm, slab_hbm, lat_hbm, lay_hbm,
     out,
     vals, rslab, rlat, rlay, force, phase, att, pml, rate_re, rate_im,
-    data, spread, arrived, right,
+    data, spread, arrived, left, right,
     prod_send, prod_all, fwd_send, gathered,
     down_send, down_recv, up_send, up_recv,
     down_back, up_back, enter_down, enter_up,
@@ -119,7 +119,7 @@
             jnp.sum((within[i * S : (i + 1) * S] + passed) * cuts[i], axis=0, keepdims=True)
         )
         passed = passed + jnp.sum(cuts[i], axis=1, keepdims=True)
-    slot = slab_of * LANES + jnp.concatenate(ranks, axis=1).astype(jnp.int32)
+    slot = slab_of * CAP + jnp.concatenate(ranks, axis=1).astype(jnp.int32)
     lateral = rlat[...]
     data[...] = jnp.zeros_like(data)
     data[0:C, :] = vals[...]
@@ -136,14 +136,14 @@
         spread[s] = routed[0:8] + routed[8:16] + routed[16:24]
         return carry
 
-    lax.fori_loop(0, S, route, 0)
+    lax.fori_loop(0, S // 2, route, 0, unroll=4)
 
     pl.semaphore_wait(barrier, S + 1)
-    arrived[me] = spread[me]
+    arrived[me] = spread[lax.div(me, 2)]
     spreads = []
     for peer in peers:
         copy = remote(
-            spread.at[peer], arrived.at[me], spread_s.at[peer], spread_r.at[me], {"slab": peer}
+            spread.at[lax.div(peer, 2)], arrived.at[me], spread_s.at[peer], spread_r.at[me], {"slab": peer}
         )
         copy.start()
         spreads.append(copy)
@@ -188,35 +188,41 @@
 
     for peer in peers:
         remote(
-            spread.at[peer], arrived.at[peer], spread_s.at[peer], spread_r.at[peer], {"slab": peer}
+            spread.at[lax.div(peer, 2)], arrived.at[peer], spread_s.at[peer], spread_r.at[peer], {"slab": peer}
         ).wait_recv()
     slots = S * CAP
-    got = jnp.concatenate(
-        [arrived[2 * i] + pltpu.roll(arrived[2 * i + 1], CAP, 1) for i in range(S // 2)], axis=1
-    )
+    low_half = lax.broadcasted_iota(jnp.int32, (8, LANES), 1) < CAP
+    keeps_low = lax.rem(me, 2) == 0
+
+    def packed(i):
+        a, b = arrived[2 * i], arrived[2 * i + 1]
+        low = jnp.where(keeps_low, a, pltpu.roll(a, CAP, 1))
+        high = jnp.where(keeps_low, pltpu.roll(b, CAP, 1), b)
+        return jnp.where(low_half, low, high)
+
+    got = jnp.concatenate([packed(i) for i in range(S // 2)], axis=1)
     row_at = got[C : C + 1, :].astype(jnp.int32)
     col_at = got[C + 1 : C + 2, :].astype(jnp.int32)
-    x_at = lax.broadcasted_iota(jnp.int32, (X, slots), 0)
+    left[...] = jnp.where(
+        lax.broadcasted_iota(jnp.int32, (L * X, slots), 0) == row_at, 1.0, 0.0
+    ).astype(BF16)
     on_col = lax.broadcasted_iota(jnp.int32, (Y, slots), 0) == col_at
     parts = [part.astype(F32) for part in thirds(got)]
-    for i in range(3):
-        for c in range(C):
-            right[c * Y : (c + 1) * Y, i * slots : (i + 1) * slots] = jnp.where(
-                on_col, parts[i][c : c + 1, :], 0.0
-            ).astype(BF16)
     loads[7].wait()
-
-    def inject(l, carry):
-        on_row = jnp.where(x_at + l * X == row_at, 1.0, 0.0).astype(BF16)
+    for s in range(shots):
+        for i in range(3):
+            for a in (0, 1):
+                c = 2 * s + a
+                right[c * Y : (c + 1) * Y, i * slots : (i + 1) * slots] = jnp.where(
+                    on_col, parts[i][c : c + 1, :], 0.0
+                ).astype(BF16)
         added = lax.dot_general(
-            jnp.concatenate([on_row] * 3, axis=1), right[...], (((1,), (1,)), ((), ())),
-            preferred_element_type=F32,
-        )
-        for c in range(C):
-            force[l, c] += added[:, c * Y : (c + 1) * Y]
-        return carry
-
-    lax.fori_loop(0, L, inject, 0)
+            jnp.concatenate([left[...]] * 3, axis=1), right[2 * s * Y : (2 * s + 2) * Y, :],
+            (((1,), (1,)), ((), ())), preferred_element_type=F32,
+        )
+        for l in range(L):
+            for a in (0, 1):
+                force[l, 2 * s + a] += added[l * X : (l + 1) * X, a * Y : (a + 1) * Y]
 
     def local(half, k, dst):
         at = pl.ds(pl.multiple_of(half * H + k * R, R), R)
@@ -444,7 +450,7 @@
     for copy in spreads + [rows_out, cols_out]:
         copy.wait_send()
 
-    def left(step, carry):
+    def drain(step, carry):
         j = fellow(step)
         prod_copy(j, m).wait_send()
         for k in range(K):
@@ -453,7 +459,7 @@
             up_back_copy(j, k, m).wait_send()
         return carry
 
-    lax.fori_loop(1, M, left, 0)
+    lax.fori_loop(1, M, drain, 0)
 
     @pl.when(g < G - 1)
     def _():
@@ -480,8 +486,8 @@
         vmem((C, rows), F32), vmem((1, rows), jnp.int32), vmem((1, rows), jnp.int32), vmem((1, rows), jnp.int32),
         vmem((L, C, X, Y), F32), vmem((L, X, Y), F32), vmem((L, X, Y), F32), vmem((X, Y), jnp.int32),
         vmem((L, X, Y), F32), vmem((L, X, Y), F32),
-        vmem((8, rows), F32), vmem((S, 8, LANES), F32), vmem((S, 8, LANES), F32),
-        vmem((C * Y, 3 * S * CAP), BF16),
+        vmem((8, rows), F32), vmem((S // 2, 8, LANES), F32), vmem((S, 8, LANES), F32),
+        vmem((L * X, S * CAP), BF16), vmem((C * Y, 3 * S * CAP), BF16),
         vmem((M, 2, H, Y), F32), vmem((M, 2, H, Y), F32),
         vmem((M, K, 2 * C, R, Y), F32), vmem((M, K, 2 * C, R, Y), F32),
         chunked, chunked, chunked, chunked, spaced, spaced, spaced, spaced,

time: 34.9 us -> 32.8 us (0.940)
  Pallas kernels: 33.8 us -> 31.7 us
    pallas_call x1, Pallas kernels: 33.8 us -> 31.7 us  [shards(): pl.pallas_call(functools.partial(kernel, (S, L, C, X, Y, K, M)), out_shap...]
where the time goes in v4:
time: 32.8 us; the launch traced here: 32.7 us
  Pallas kernels  31.7 us (97%)
  local copies, waits for them, and re-layouts  0.97 us (3%)
    pallas_call x1, Pallas kernels, shards(): pl.pallas_call(functools.partial(kernel, (S, L, C, X, Y, K, M)), out_shap...  31.7 us
    unnamed x1, local copies, waits for them, and re-layouts  0.97 us

profile of v4, /device:TPU:0, one launch (start us, length us, event | category | flops | bytes accessed | tf_op | source)
XLA Modules:
  0.0 32.7 jit_solution(13395555296630545635)
XLA Ops:
  0.0 31.7 %shard_map.82 = f32[4,4,128,128]{3,2,1,0:T(8,128)S(1)} custom-call(f32[4,4,128,128]{3,2,1,0:T(8,128)} %src_hbm.1, f32[4,128,128]{2,1,0:T(8,128)} %phase_hbm.1, f32[4,128,128]{2,1,0:T(8,128)} %att_hbm.1, s32[128,128]{1,0:T(8,128)} %pml_hbm.1, f32[4,512]{1,0:T(4,128)} %bitcast.4, s32[1,512]{1,0:T(1,128)} %bitcast.5, s32[1,512]{1,0:T(1,128)} %bitcast.6, ...), custom_call_target="tpu_custom_call" | custom-call | tf_op jit(solution)/shard_map/pallas_call | solution.py:503
  31.7 1.0 %copy.10 = f32[4,4,128,128]{3,2,1,0:T(8,128)} copy(f32[4,4,128,128]{3,2,1,0:T(8,128)S(1)} %shard_map.82) | data formatting | bytes 2097152

commit v5 on v4

--- a/solution.py
+++ b/solution.py
@@ -8,7 +8,7 @@
 from jax.sharding import PartitionSpec as P
 
 GROUP = 4
-CHUNKS = 2
+CHUNKS = 4
 LANES = 128
 CAP = 64
 VMEM_BYTES = 48 * 1024 * 1024

time: 32.8 us -> 36.4 us (1.11)
  Pallas kernels: 31.7 us -> 35.3 us
    pallas_call x1, Pallas kernels: 31.7 us -> 35.3 us  [shards(): pl.pallas_call(functools.partial(kernel, (S, L, C, X, Y, K, M)), out_shap...]
where the time goes in v5:
time: 36.4 us; the launch traced here: 36.3 us
  Pallas kernels  35.3 us (97%)
  local copies, waits for them, and re-layouts  0.97 us (3%)
    pallas_call x1, Pallas kernels, shards(): pl.pallas_call(functools.partial(kernel, (S, L, C, X, Y, K, M)), out_shap...  35.3 us
    unnamed x1, local copies, waits for them, and re-layouts  0.97 us

profile of v5, /device:TPU:0, one launch (start us, length us, event | category | flops | bytes accessed | tf_op | source)
XLA Modules:
  0.0 36.3 jit_solution(15546770408741513211)
XLA Ops:
  0.0 35.3 %shard_map.82 = f32[4,4,128,128]{3,2,1,0:T(8,128)S(1)} custom-call(f32[4,4,128,128]{3,2,1,0:T(8,128)} %src_hbm.1, f32[4,128,128]{2,1,0:T(8,128)} %phase_hbm.1, f32[4,128,128]{2,1,0:T(8,128)} %att_hbm.1, s32[128,128]{1,0:T(8,128)} %pml_hbm.1, f32[4,512]{1,0:T(4,128)} %bitcast.4, s32[1,512]{1,0:T(1,128)} %bitcast.5, s32[1,512]{1,0:T(1,128)} %bitcast.6, ...), custom_call_target="tpu_custom_call" | custom-call | tf_op jit(solution)/shard_map/pallas_call | solution.py:503
  35.3 1.0 %copy.10 = f32[4,4,128,128]{3,2,1,0:T(8,128)} copy(f32[4,4,128,128]{3,2,1,0:T(8,128)S(1)} %shard_map.82) | data formatting | bytes 2097152

commit v6 on v4

--- a/solution.py
+++ b/solution.py
@@ -64,7 +64,6 @@
     py = lax.axis_index("py")
     g = lax.div(me, M)
     m = lax.rem(me, M)
-    fellows = M - 1
     other_x = {"px": 1 - px}
     other_y = {"py": 1 - py}
 
@@ -248,17 +247,20 @@
             place_of(j),
         )
 
-    def give(i, carry):
-        k, j = lax.div(i, fellows), fellow(1 + lax.rem(i, fellows))
-        local(j, k, fwd_send.at[j, k])
-        fwd_copy(j, k, m).start()
+    others = [fellow(step) for step in range(1, M)]
+
+    def give(k, carry):
+        for j in others:
+            local(j, k, fwd_send.at[j, k])
+        for j in others:
+            fwd_copy(j, k, m).start()
         return carry
 
     def keep(k, carry):
         local(m, k, gathered.at[m, k])
         return carry
 
-    lax.fori_loop(0, K * fellows, give, 0)
+    lax.fori_loop(0, K, give, 0)
     lax.fori_loop(0, K, keep, 0)
 
     pad = comb.shape[1] // 2 - X // 2
@@ -392,14 +394,15 @@
 
     lax.fori_loop(0, K + G - 1, chain, 0)
 
-    def finish(i, carry):
-        k, j = lax.div(i, fellows), fellow(1 + lax.rem(i, fellows))
-        down_back_copy(j, k, j).wait_recv()
-        up_back_copy(j, k, j).wait_recv()
-        full(j, k)
-        return carry
-
-    lax.fori_loop(0, K * fellows, finish, 0)
+    def finish(k, carry):
+        for j in others:
+            down_back_copy(j, k, j).wait_recv()
+            up_back_copy(j, k, j).wait_recv()
+        for j in others:
+            full(j, k)
+        return carry
+
+    lax.fori_loop(0, K, finish, 0)
 
     cols_out = remote(col_send, col_recv, col_s, col_r, other_y)
     cols_out.start()

time: 32.8 us -> 32.9 us (level)
  no operation moved by 1% of the time
where the time goes in v6:
time: 32.9 us; the launch traced here: 32.8 us
  Pallas kernels  31.8 us (97%)
  local copies, waits for them, and re-layouts  0.97 us (3%)
    pallas_call x1, Pallas kernels, shards(): pl.pallas_call(functools.partial(kernel, (S, L, C, X, Y, K, M)), out_shap...  31.8 us
    unnamed x1, local copies, waits for them, and re-layouts  0.97 us

profile of v6, /device:TPU:0, one launch (start us, length us, event | category | flops | bytes accessed | tf_op | source)
XLA Modules:
  0.0 32.8 jit_solution(17192454144493567212)
XLA Ops:
  0.0 31.8 %shard_map.82 = f32[4,4,128,128]{3,2,1,0:T(8,128)S(1)} custom-call(f32[4,4,128,128]{3,2,1,0:T(8,128)} %src_hbm.1, f32[4,128,128]{2,1,0:T(8,128)} %phase_hbm.1, f32[4,128,128]{2,1,0:T(8,128)} %att_hbm.1, s32[128,128]{1,0:T(8,128)} %pml_hbm.1, f32[4,512]{1,0:T(4,128)} %bitcast.4, s32[1,512]{1,0:T(1,128)} %bitcast.5, s32[1,512]{1,0:T(1,128)} %bitcast.6, ...), custom_call_target="tpu_custom_call" | custom-call | tf_op jit(solution)/shard_map/pallas_call | solution.py:506
  31.8 1.0 %copy.10 = f32[4,4,128,128]{3,2,1,0:T(8,128)} copy(f32[4,4,128,128]{3,2,1,0:T(8,128)S(1)} %shard_map.82) | data formatting | bytes 2097152

commit v7 on v5

--- a/solution.py
+++ b/solution.py
@@ -8,7 +8,7 @@
 from jax.sharding import PartitionSpec as P
 
 GROUP = 4
-CHUNKS = 4
+CHUNKS = 1
 LANES = 128
 CAP = 64
 VMEM_BYTES = 48 * 1024 * 1024

time: 36.4 us -> 31.7 us (0.87)
  Pallas kernels: 35.3 us -> 30.6 us
    pallas_call x1, Pallas kernels: 35.3 us -> 30.6 us  [shards(): pl.pallas_call(functools.partial(kernel, (S, L, C, X, Y, K, M)), out_shap...]
where the time goes in v7:
time: 31.7 us; the launch traced here: 31.5 us
  Pallas kernels  30.6 us (97%)
  local copies, waits for them, and re-layouts  0.97 us (3%)
    pallas_call x1, Pallas kernels, shards(): pl.pallas_call(functools.partial(kernel, (S, L, C, X, Y, K, M)), out_shap...  30.6 us
    unnamed x1, local copies, waits for them, and re-layouts  0.97 us

profile of v7, /device:TPU:0, one launch (start us, length us, event | category | flops | bytes accessed | tf_op | source)
XLA Modules:
  0.0 31.5 jit_solution(10723264220628731211)
XLA Ops:
  0.0 30.6 %shard_map.82 = f32[4,4,128,128]{3,2,1,0:T(8,128)S(1)} custom-call(f32[4,4,128,128]{3,2,1,0:T(8,128)} %src_hbm.1, f32[4,128,128]{2,1,0:T(8,128)} %phase_hbm.1, f32[4,128,128]{2,1,0:T(8,128)} %att_hbm.1, s32[128,128]{1,0:T(8,128)} %pml_hbm.1, f32[4,512]{1,0:T(4,128)} %bitcast.4, s32[1,512]{1,0:T(1,128)} %bitcast.5, s32[1,512]{1,0:T(1,128)} %bitcast.6, ...), custom_call_target="tpu_custom_call" | custom-call | tf_op jit(solution)/shard_map/pallas_call | solution.py:503
  30.6 1.0 %copy.10 = f32[4,4,128,128]{3,2,1,0:T(8,128)} copy(f32[4,4,128,128]{3,2,1,0:T(8,128)S(1)} %shard_map.82) | data formatting | bytes 2097152

commit v8 on v7

--- a/solution.py
+++ b/solution.py
@@ -69,7 +69,9 @@
     other_y = {"py": 1 - py}
 
     def fellow(step):
-        return lax.rem(m + step, M)
+        first = lax.rem(lax.div(m, 2) + step % 2, 2)
+        second = lax.rem(lax.rem(m, 2) + (M - step) // 2, 2)
+        return 2 * first + second
 
     def place_of(member):
         return {"slab": g * M + member}
@@ -393,7 +395,7 @@
     lax.fori_loop(0, K + G - 1, chain, 0)
 
     def finish(i, carry):
-        k, j = lax.div(i, fellows), fellow(1 + lax.rem(i, fellows))
+        k, j = lax.div(i, fellows), fellow(fellows - lax.rem(i, fellows))
         down_back_copy(j, k, j).wait_recv()
         up_back_copy(j, k, j).wait_recv()
         full(j, k)

time: 31.7 us -> 31.6 us (level)
  no operation moved by 1% of the time
where the time goes in v8:
time: 31.6 us; the launch traced here: 31.4 us
  Pallas kernels  30.5 us (97%)
  local copies, waits for them, and re-layouts  0.97 us (3%)
    pallas_call x1, Pallas kernels, shards(): pl.pallas_call(functools.partial(kernel, (S, L, C, X, Y, K, M)), out_shap...  30.5 us
    unnamed x1, local copies, waits for them, and re-layouts  0.97 us

profile of v8, /device:TPU:0, one launch (start us, length us, event | category | flops | bytes accessed | tf_op | source)
XLA Modules:
  0.0 31.4 jit_solution(5223090916393044210)
XLA Ops:
  0.0 30.5 %shard_map.82 = f32[4,4,128,128]{3,2,1,0:T(8,128)S(1)} custom-call(f32[4,4,128,128]{3,2,1,0:T(8,128)} %src_hbm.1, f32[4,128,128]{2,1,0:T(8,128)} %phase_hbm.1, f32[4,128,128]{2,1,0:T(8,128)} %att_hbm.1, s32[128,128]{1,0:T(8,128)} %pml_hbm.1, f32[4,512]{1,0:T(4,128)} %bitcast.4, s32[1,512]{1,0:T(1,128)} %bitcast.5, s32[1,512]{1,0:T(1,128)} %bitcast.6, ...), custom_call_target="tpu_custom_call" | custom-call | tf_op jit(solution)/shard_map/pallas_call | solution.py:505
  30.5 1.0 %copy.10 = f32[4,4,128,128]{3,2,1,0:T(8,128)} copy(f32[4,4,128,128]{3,2,1,0:T(8,128)S(1)} %shard_map.82) | data formatting | bytes 2097152
